TPU v7x, 32 devices: a whole 2x2x4 slice. The times are simulated.
32 devices in a mesh: ctx: 8 (over y, x, core), fsdp: 4 (over z).
Axes of the slice: x: 2, y: 2, z: 4, core: 2. Of those that a mesh axis runs over, the one named last changes fastest.
Arguments:
- hidden: bfloat16 [8, 2, 4, 64, 1024], P('ctx', None, 'fsdp'), may hold values from -6 to 6
- block_order: int32 [8, 2], replicated, may hold values from 0 to 15, as said below
- alibi_slopes: float32 [16], replicated, may hold values from 6.1035156e-05 to 0.05
- ln1_gain: bfloat16 [1024], P('fsdp'), may hold values from 0.25 to 1.75
- ln1_bias: bfloat16 [1024], P('fsdp'), may hold values from -4 to 4
- w_qkv: bfloat16 [1024, 3072], P('fsdp'), may hold values from -0.1875 to 0.1875
- qv_bias: bfloat16 [16, 128], P('fsdp'), may hold values from -4 to 4
- w_out: bfloat16 [1024, 1024], P('fsdp'), may hold values from -2 to 2
- out_bias: bfloat16 [1024], P('fsdp'), may hold values from -4 to 4
- ln2_gain: bfloat16 [1024], P('fsdp'), may hold values from 0.25 to 1.75
- ln2_bias: bfloat16 [1024], P('fsdp'), may hold values from -4 to 4
- w_up: bfloat16 [1024, 4096], P('fsdp'), may hold values from -0.1875 to 0.1875
- up_bias: bfloat16 [4096], P('fsdp'), may hold values from -4 to 4
- w_down: bfloat16 [4096, 1024], P('fsdp'), may hold values from -0.09375 to 0.09375
- down_bias: bfloat16 [1024], P('fsdp'), may hold values from -4 to 4
- d_output: bfloat16 [8, 2, 4, 64, 1024], P('ctx', None, 'fsdp'), may hold values from -6 to 6
Outputs:
- output: bfloat16 [8, 2, 4, 64, 1024], P('ctx', None, 'fsdp')
- d_hidden: bfloat16 [8, 2, 4, 64, 1024], P('ctx', None, 'fsdp')
- d_ln1_gain: float32 [1024], P('fsdp')
- d_ln1_bias: float32 [1024], P('fsdp')
- d_w_qkv: float32 [1024, 3072], P('fsdp')
- d_qv_bias: float32 [16, 128], P('fsdp')
- d_w_out: float32 [1024, 1024], P('fsdp')
- d_out_bias: float32 [1024], P('fsdp')
- d_ln2_gain: float32 [1024], P('fsdp')
- d_ln2_bias: float32 [1024], P('fsdp')
- d_w_up: float32 [1024, 4096], P('fsdp')
- d_up_bias: float32 [4096], P('fsdp')
- d_w_down: float32 [4096, 1024], P('fsdp')
- d_down_bias: float32 [1024], P('fsdp')
Inputs may be any that keep to these rules, and one draw needn't show every extreme that they name: block_order names every block 0 to 15 once, and each row holds two blocks whose numbers add up to 15.
All inputs are finite; a program needn't handle non-finite values.
Results may differ from a plain program's by a relative error of at most 0.038.
Values may be sent and summed in bfloat16 or wider, within the bound.
A program may use at most 192 MiB of HBM per device.

v0:
```python
import math

import jax
import jax.numpy as jnp
from jax import lax
from jax.sharding import PartitionSpec as P

EPSILON = 1e-05
NEGATIVE = -1e30
TANH_SCALE = 0.7978845608028654


def gelu_tanh(values):
    return (
        0.5 * values * (1.0 + jnp.tanh(TANH_SCALE * (values + 0.044715 * values * values * values)))
    )


def norm_parts(rows_in):
    centred = rows_in - jnp.mean(rows_in, axis=-1, keepdims=True)
    inv_std = lax.rsqrt(jnp.mean(centred * centred, axis=-1, keepdims=True) + EPSILON)
    return (centred * inv_std, inv_std)


def norm_back(d_norm, gain, normed, inv_std):
    scaled = d_norm * gain
    return inv_std * (
        scaled
        - jnp.mean(scaled, axis=-1, keepdims=True)
        - normed * jnp.mean(scaled * normed, axis=-1, keepdims=True)
    )


def token_places(block_order, first_row, row_total, tok_rows, half_rows, group_count):
    index_rows = first_row + jnp.arange(row_total, dtype=jnp.int32)
    span_rows = tok_rows * group_count
    ctx_rows = index_rows // span_rows
    rest_rows = index_rows % span_rows
    group_rows = rest_rows // tok_rows
    slot_rows = rest_rows % tok_rows // half_rows
    inner_rows = rest_rows % half_rows
    flat_order = block_order.reshape(-1)
    lookup = ctx_rows * 2 + slot_rows
    table_ids = jnp.arange(flat_order.shape[0], dtype=jnp.int32)
    block_ids = jnp.sum(
        jnp.where(lookup[:, None] == table_ids[None, :], flat_order[None, :], 0), axis=1
    )
    return block_ids * (half_rows * group_count) + group_rows * half_rows + inner_rows


def scores_of(query_rows, query_pos, key_rows, key_pos, slopes, score_scale):
    raw_score = (
        jnp.einsum("qhd,khd->hqk", query_rows, key_rows, preferred_element_type=jnp.float32)
        * score_scale
    )
    pos_gap = (query_pos[:, None] - key_pos[None, :]).astype(jnp.float32)
    raw_score = raw_score - slopes[:, None, None] * pos_gap[None]
    allowed = (key_pos[None, :] <= query_pos[:, None])[None]
    return (jnp.where(allowed, raw_score, NEGATIVE), allowed)


def split_blocks(array_in, block_rows):
    return array_in.reshape((array_in.shape[0] // block_rows, block_rows) + array_in.shape[1:])


def local(
    hidden,
    block_order,
    alibi_slopes,
    ln1_gain,
    ln1_bias,
    w_qkv,
    qv_bias,
    w_out,
    out_bias,
    ln2_gain,
    ln2_bias,
    w_up,
    up_bias,
    w_down,
    down_bias,
    d_output,
):
    half_rows = hidden.shape[3]
    width = hidden.shape[4]
    tok_rows = 2 * half_rows
    group_count = lax.axis_size("fsdp")
    head_count = alibi_slopes.shape[0]
    head_width = width // head_count
    local_heads = head_count // group_count
    span_rows = tok_rows * group_count
    score_scale = 1.0 / math.sqrt(head_width)
    ctx_index = lax.axis_index("ctx")
    group_index = lax.axis_index("fsdp")
    slopes = lax.dynamic_slice_in_dim(alibi_slopes, group_index * local_heads, local_heads)

    def places(first_row, row_total):
        return token_places(block_order, first_row, row_total, tok_rows, half_rows, group_count)

    query_pos = places(ctx_index * span_rows, span_rows)
    gathered = (
        lax.all_gather(w_qkv, "fsdp", axis=0, tiled=True),
        lax.all_gather(w_out, "fsdp", axis=0, tiled=True),
        lax.all_gather(w_up, "fsdp", axis=0, tiled=True),
        lax.all_gather(w_down, "fsdp", axis=0, tiled=True),
        lax.all_gather(qv_bias, "fsdp", axis=0, tiled=True),
        lax.all_gather(ln1_gain, "fsdp", axis=0, tiled=True),
        lax.all_gather(ln1_bias, "fsdp", axis=0, tiled=True),
        lax.all_gather(out_bias, "fsdp", axis=0, tiled=True),
        lax.all_gather(ln2_gain, "fsdp", axis=0, tiled=True),
        lax.all_gather(ln2_bias, "fsdp", axis=0, tiled=True),
        lax.all_gather(up_bias, "fsdp", axis=0, tiled=True),
        lax.all_gather(down_bias, "fsdp", axis=0, tiled=True),
    )
    (
        full_qkv,
        full_out,
        full_up,
        full_down,
        full_qv,
        full_g1,
        full_b1,
        full_bo,
        full_g2,
        full_b2,
        full_bu,
        full_bd,
    ) = gathered
    rows_in = hidden.reshape(tok_rows, width).astype(jnp.float32)
    normed_one, inv_one = norm_parts(rows_in)
    first_in = (normed_one * full_g1.astype(jnp.float32) + full_b1.astype(jnp.float32)).astype(
        jnp.bfloat16
    )
    zero_bias = jnp.zeros((head_count, head_width), jnp.bfloat16)
    joined_bias = (
        jnp.concatenate([full_qv[:, :head_width], zero_bias, full_qv[:, head_width:]], axis=1)
        .reshape(3 * width)
        .astype(jnp.float32)
    )
    joined = (jnp.dot(first_in, full_qkv, preferred_element_type=jnp.float32) + joined_bias).astype(
        jnp.bfloat16
    )
    joined_heads = lax.all_to_all(
        joined.reshape(tok_rows, group_count, local_heads * 3 * head_width),
        "fsdp",
        split_axis=1,
        concat_axis=0,
        tiled=True,
    )
    joined_heads = joined_heads.reshape(span_rows, local_heads, 3, head_width)
    queries = joined_heads[:, :, 0]
    local_keys = joined_heads[:, :, 1]
    local_values = joined_heads[:, :, 2]
    key_values = (
        joined_heads[:, :, 1:]
        .transpose(0, 2, 1, 3)
        .reshape(span_rows, 2 * local_heads * head_width)
    )
    start_state = (
        jnp.full((local_heads, span_rows), NEGATIVE, jnp.float32),
        jnp.zeros((local_heads, span_rows), jnp.float32),
        jnp.zeros((local_heads, span_rows, head_width), jnp.float32),
    )
    kv_piece = lax.all_gather(key_values, "ctx", axis=0, tiled=True)
    row_total = kv_piece.shape[0]
    key_block = math.gcd(row_total, 512)
    key_pos = places(jnp.int32(0), row_total)
    kv_blocks = split_blocks(kv_piece.reshape(row_total, 2, local_heads, head_width), key_block)

    def forward_key_step(state_now, block_item):
        run_max, run_sum, run_out = state_now
        kv_rows, pos_rows = block_item
        raw_score, allowed = scores_of(
            queries, query_pos, kv_rows[:, 0], pos_rows, slopes, score_scale
        )
        new_max = jnp.maximum(run_max, jnp.max(raw_score, axis=-1))
        weights_exp = jnp.where(allowed, jnp.exp(raw_score - new_max[..., None]), 0.0)
        shrink = jnp.exp(run_max - new_max)
        run_sum = run_sum * shrink + jnp.sum(weights_exp, axis=-1)
        run_out = run_out * shrink[..., None] + jnp.einsum(
            "hqk,khd->hqd",
            weights_exp.astype(jnp.bfloat16),
            kv_rows[:, 1],
            preferred_element_type=jnp.float32,
        )
        return ((new_max, run_sum, run_out), None)

    final_state, unused = lax.scan(
        forward_key_step, start_state, (kv_blocks, split_blocks(key_pos, key_block))
    )
    run_max, run_sum, run_out = final_state
    out_heads = run_out / run_sum[..., None]
    log_sums = run_max + jnp.log(run_sum)
    heads_sent = (
        out_heads.astype(jnp.bfloat16)
        .transpose(1, 0, 2)
        .reshape(group_count, tok_rows, local_heads * head_width)
    )
    attended = lax.all_to_all(heads_sent, "fsdp", split_axis=0, concat_axis=2, tiled=True).reshape(
        tok_rows, width
    )
    middle = (
        rows_in
        + jnp.dot(attended, full_out, preferred_element_type=jnp.float32)
        + full_bo.astype(jnp.float32)
    )
    normed_two, inv_two = norm_parts(middle)
    second_in = (normed_two * full_g2.astype(jnp.float32) + full_b2.astype(jnp.float32)).astype(
        jnp.bfloat16
    )
    hidden_pre = jnp.dot(second_in, full_up, preferred_element_type=jnp.float32) + full_bu.astype(
        jnp.float32
    )
    activated, gelu_pull = jax.vjp(gelu_tanh, hidden_pre)
    activated = activated.astype(jnp.bfloat16)
    result = (
        middle
        + jnp.dot(activated, full_down, preferred_element_type=jnp.float32)
        + full_bd.astype(jnp.float32)
    )
    output = result.astype(jnp.bfloat16).reshape(hidden.shape)
    back_qkv, back_out, back_up, back_down, back_g1, back_g2 = (
        lax.all_gather(w_qkv, "fsdp", axis=0, tiled=True),
        lax.all_gather(w_out, "fsdp", axis=0, tiled=True),
        lax.all_gather(w_up, "fsdp", axis=0, tiled=True),
        lax.all_gather(w_down, "fsdp", axis=0, tiled=True),
        lax.all_gather(ln1_gain, "fsdp", axis=0, tiled=True),
        lax.all_gather(ln2_gain, "fsdp", axis=0, tiled=True),
    )
    grad_out = d_output.reshape(tok_rows, width)
    grad_out_f = grad_out.astype(jnp.float32)
    grad_act = jnp.dot(grad_out, back_down.T, preferred_element_type=jnp.float32).astype(
        jnp.bfloat16
    )
    grad_pre = gelu_pull(grad_act.astype(jnp.float32))[0].astype(jnp.bfloat16)
    grad_second = jnp.dot(grad_pre, back_up.T, preferred_element_type=jnp.float32)
    grad_middle = grad_out_f + norm_back(
        grad_second, back_g2.astype(jnp.float32), normed_two, inv_two
    )
    grad_branch = grad_middle.astype(jnp.bfloat16)
    grad_attended = jnp.dot(grad_branch, back_out.T, preferred_element_type=jnp.float32).astype(
        jnp.bfloat16
    )
    grad_heads = lax.all_to_all(
        grad_attended.reshape(tok_rows, group_count, local_heads * head_width),
        "fsdp",
        split_axis=1,
        concat_axis=0,
        tiled=True,
    )
    grad_heads = grad_heads.reshape(span_rows, local_heads, head_width)
    delta_rows = jnp.sum(grad_heads.astype(jnp.float32).transpose(1, 0, 2) * out_heads, axis=-1)
    kv_piece = lax.all_gather(key_values, "ctx", axis=0, tiled=True)
    row_total = kv_piece.shape[0]
    key_block = math.gcd(row_total, 512)
    key_pos = places(jnp.int32(0), row_total)
    kv_blocks = split_blocks(kv_piece.reshape(row_total, 2, local_heads, head_width), key_block)

    def query_key_step(grad_now, block_item):
        kv_rows, pos_rows = block_item
        raw_score, allowed = scores_of(
            queries, query_pos, kv_rows[:, 0], pos_rows, slopes, score_scale
        )
        soft_probs = jnp.where(allowed, jnp.exp(raw_score - log_sums[..., None]), 0.0)
        grad_probs = jnp.einsum(
            "qhd,khd->hqk", grad_heads, kv_rows[:, 1], preferred_element_type=jnp.float32
        )
        grad_score = (soft_probs * (grad_probs - delta_rows[..., None])).astype(jnp.bfloat16)
        grad_now = (
            grad_now
            + jnp.einsum(
                "hqk,khd->hqd", grad_score, kv_rows[:, 0], preferred_element_type=jnp.float32
            )
            * score_scale
        )
        return (grad_now, None)

    grad_final, unused = lax.scan(
        query_key_step,
        jnp.zeros((local_heads, span_rows, head_width), jnp.float32),
        (kv_blocks, split_blocks(key_pos, key_block)),
    )
    pair_rows = jnp.stack([queries, grad_heads], axis=1).reshape(
        span_rows, 2 * local_heads * head_width
    )
    zero_heads = jnp.zeros((local_heads, span_rows, head_width), jnp.float32)
    grad_key = zero_heads
    grad_value = zero_heads
    pair_piece = lax.all_gather(pair_rows, "ctx", axis=0, tiled=True)
    lse_piece = lax.all_gather(log_sums.T.astype(jnp.bfloat16), "ctx", axis=0, tiled=True).astype(
        jnp.float32
    )
    delta_piece = lax.all_gather(
        delta_rows.T.astype(jnp.bfloat16), "ctx", axis=0, tiled=True
    ).astype(jnp.float32)
    row_total = pair_piece.shape[0]
    query_block = math.gcd(row_total, 512)
    piece_pos = places(jnp.int32(0), row_total)
    pair_blocks = split_blocks(
        pair_piece.reshape(row_total, 2, local_heads, head_width), query_block
    )

    def query_step(grads_now, block_item):
        key_now, value_now = grads_now
        pair_now, pos_now, lse_now, delta_now = block_item
        raw_score, allowed = scores_of(
            pair_now[:, 0], pos_now, local_keys, query_pos, slopes, score_scale
        )
        soft_probs = jnp.where(allowed, jnp.exp(raw_score - lse_now.T[..., None]), 0.0)
        value_now = value_now + jnp.einsum(
            "hqk,qhd->hkd",
            soft_probs.astype(jnp.bfloat16),
            pair_now[:, 1],
            preferred_element_type=jnp.float32,
        )
        grad_probs = jnp.einsum(
            "qhd,khd->hqk", pair_now[:, 1], local_values, preferred_element_type=jnp.float32
        )
        grad_score = (soft_probs * (grad_probs - delta_now.T[..., None])).astype(jnp.bfloat16)
        key_now = (
            key_now
            + jnp.einsum(
                "hqk,qhd->hkd", grad_score, pair_now[:, 0], preferred_element_type=jnp.float32
            )
            * score_scale
        )
        return ((key_now, value_now), None)

    items = (
        pair_blocks,
        split_blocks(piece_pos, query_block),
        split_blocks(lse_piece, query_block),
        split_blocks(delta_piece, query_block),
    )
    grads_final, unused = lax.scan(query_step, (grad_key, grad_value), items)
    grad_key, grad_value = grads_final
    grad_joined_heads = (
        jnp.stack([grad_final, grad_key, grad_value], axis=2)
        .transpose(1, 0, 2, 3)
        .astype(jnp.bfloat16)
    )
    grad_joined_heads = grad_joined_heads.reshape(
        group_count, tok_rows, local_heads * 3 * head_width
    )
    grad_joined = lax.all_to_all(
        grad_joined_heads, "fsdp", split_axis=0, concat_axis=2, tiled=True
    ).reshape(tok_rows, 3 * width)
    grad_first = jnp.dot(grad_joined, back_qkv.T, preferred_element_type=jnp.float32)
    grad_rows = grad_middle + norm_back(
        grad_first, back_g1.astype(jnp.float32), normed_one, inv_one
    )
    d_hidden = grad_rows.astype(jnp.bfloat16).reshape(hidden.shape)
    joined_sums = jnp.sum(grad_joined.astype(jnp.float32), axis=0).reshape(
        head_count, 3, head_width
    )
    sum_qv = jnp.concatenate([joined_sums[:, 0], joined_sums[:, 2]], axis=1)
    sum_g1 = jnp.sum(grad_first * normed_one, axis=0)
    sum_b1 = jnp.sum(grad_first, axis=0)
    sum_bo = jnp.sum(grad_branch.astype(jnp.float32), axis=0)
    sum_g2 = jnp.sum(grad_second * normed_two, axis=0)
    sum_b2 = jnp.sum(grad_second, axis=0)
    sum_bu = jnp.sum(grad_pre.astype(jnp.float32), axis=0)
    sum_bd = jnp.sum(grad_out_f, axis=0)
    small_sums = (
        lax.psum_scatter(
            sum_g1.astype(jnp.bfloat16), "fsdp", scatter_dimension=0, tiled=True
        ).astype(jnp.float32),
        lax.psum_scatter(
            sum_b1.astype(jnp.bfloat16), "fsdp", scatter_dimension=0, tiled=True
        ).astype(jnp.float32),
        lax.psum_scatter(
            sum_qv.astype(jnp.bfloat16), "fsdp", scatter_dimension=0, tiled=True
        ).astype(jnp.float32),
        lax.psum_scatter(
            sum_bo.astype(jnp.bfloat16), "fsdp", scatter_dimension=0, tiled=True
        ).astype(jnp.float32),
        lax.psum_scatter(
            sum_g2.astype(jnp.bfloat16), "fsdp", scatter_dimension=0, tiled=True
        ).astype(jnp.float32),
        lax.psum_scatter(
            sum_b2.astype(jnp.bfloat16), "fsdp", scatter_dimension=0, tiled=True
        ).astype(jnp.float32),
        lax.psum_scatter(
            sum_bu.astype(jnp.bfloat16), "fsdp", scatter_dimension=0, tiled=True
        ).astype(jnp.float32),
        lax.psum_scatter(
            sum_bd.astype(jnp.bfloat16), "fsdp", scatter_dimension=0, tiled=True
        ).astype(jnp.float32),
    )
    term_qkv = jnp.einsum("tc,tk->ck", first_in, grad_joined, preferred_element_type=jnp.float32)
    term_out = jnp.einsum("tc,tk->ck", attended, grad_branch, preferred_element_type=jnp.float32)
    term_up = jnp.einsum("tc,tk->ck", second_in, grad_pre, preferred_element_type=jnp.float32)
    feature_part = lax.psum_scatter(
        jnp.concatenate([term_qkv, term_out, term_up], axis=1).astype(jnp.bfloat16),
        "fsdp",
        scatter_dimension=0,
        tiled=True,
    )
    down_part = lax.psum_scatter(
        jnp.einsum("tc,tk->ck", activated, grad_out, preferred_element_type=jnp.float32).astype(
            jnp.bfloat16
        ),
        "fsdp",
        scatter_dimension=0,
        tiled=True,
    )
    summed = (
        lax.psum(feature_part, "ctx").astype(jnp.float32),
        lax.psum(down_part, "ctx").astype(jnp.float32),
        lax.psum(small_sums[0].astype(jnp.bfloat16), "ctx").astype(jnp.float32),
        lax.psum(small_sums[1].astype(jnp.bfloat16), "ctx").astype(jnp.float32),
        lax.psum(small_sums[2].astype(jnp.bfloat16), "ctx").astype(jnp.float32),
        lax.psum(small_sums[3].astype(jnp.bfloat16), "ctx").astype(jnp.float32),
        lax.psum(small_sums[4].astype(jnp.bfloat16), "ctx").astype(jnp.float32),
        lax.psum(small_sums[5].astype(jnp.bfloat16), "ctx").astype(jnp.float32),
        lax.psum(small_sums[6].astype(jnp.bfloat16), "ctx").astype(jnp.float32),
        lax.psum(small_sums[7].astype(jnp.bfloat16), "ctx").astype(jnp.float32),
    )
    (
        feature_sum,
        down_sum,
        d_ln1_gain,
        d_ln1_bias,
        d_qv_bias,
        d_out_bias,
        d_ln2_gain,
        d_ln2_bias,
        d_up_bias,
        d_down_bias,
    ) = summed
    d_w_qkv = feature_sum[:, : 3 * width]
    d_w_out = feature_sum[:, 3 * width : 4 * width]
    d_w_up = feature_sum[:, 4 * width :]
    return (
        output,
        d_hidden,
        d_ln1_gain,
        d_ln1_bias,
        d_w_qkv,
        d_qv_bias,
        d_w_out,
        d_out_bias,
        d_ln2_gain,
        d_ln2_bias,
        d_w_up,
        d_up_bias,
        down_sum,
        d_down_bias,
    )


def solution(mesh):
    placed = (
        P("ctx", None, "fsdp", None, None),
        P(),
        P(),
        P("fsdp"),
        P("fsdp"),
        P("fsdp", None),
        P("fsdp", None),
        P("fsdp", None),
        P("fsdp"),
        P("fsdp"),
        P("fsdp"),
        P("fsdp", None),
        P("fsdp"),
        P("fsdp", None),
        P("fsdp"),
        P("ctx", None, "fsdp", None, None),
    )
    return jax.shard_map(
        local,
        mesh=mesh,
        in_specs=placed,
        out_specs=(
            P("ctx", None, "fsdp", None, None),
            P("ctx", None, "fsdp", None, None),
            P("fsdp"),
            P("fsdp"),
            P("fsdp", None),
            P("fsdp", None),
            P("fsdp", None),
            P("fsdp"),
            P("fsdp"),
            P("fsdp"),
            P("fsdp", None),
            P("fsdp"),
            P("fsdp", None),
            P("fsdp"),
        ),
        check_vma=False,
    )
```

profile of v0, /device:TPU:0, one launch (start us, length us, event | category | flops | bytes accessed | tf_op | source)
XLA Modules:
  0.0 1259.6 jit_solution(6409033145369920816)
XLA Ops:
  8.6 12.6 %all-gather.1 = bf16[4,1,256]{2,1,0:T(2,128)(2,1)S(1)} all-gather(bf16[1,1,256]{2,1,0:T(2,128)(2,1)S(1)} %reshape.514), channel_id=1, replica_groups=mesh['ctx'=8,'fsdp'=4] {'fsdp'}, dimensions={0}, use_global_device_ids=true | all-gather | bytes 2560 | tf_op jit(solution)/shard_map/all_gather | solution.py:108
  21.9 7.8 all-gather
  32.2 12.7 %all-gather.2 = bf16[4,4,128]{2,1,0:T(4,128)(2,1)S(1)} all-gather(bf16[1,4,128]{2,1,0:T(4,128)(2,1)} %bitcast.315), channel_id=1, replica_groups=mesh['ctx'=8,'fsdp'=4] {'fsdp'}, dimensions={0}, use_global_device_ids=true | all-gather | bytes 5120 | tf_op jit(solution)/shard_map/all_gather | solution.py:106
  46.4 81.4 %all-gather.14.cloned.1.call-done = bf16[1024,3072]{1,0:T(8,128)(2,1)} async-done(((bf16[256,3072]{1,0:T(8,128)(2,1)}), bf16[1024,3072]{1,0:T(8,128)(2,1)}) %all-gather.14.cloned.1.call-update) | async-done | bytes 6291472 | tf_op jit(solution)/shard_map/all_gather | solution.py:102
  127.7 3.8 fusion.43
  131.9 23.0 %all_to_all.60 = bf16[128,4,768]{0,2,1:T(8,128)(2,1)S(1)} all-to-all(bf16[128,4,768]{0,2,1:T(8,128)(2,1)S(1)} %bitcast.278), channel_id=1, replica_groups=mesh['ctx'=8,'fsdp'=4] {'fsdp'}, dimensions={1} | all-to-all | bytes 1572864 | tf_op jit(solution)/shard_map/all_to_all | solution.py:143
  160.2 33.2 %all-gather.16.cloned.1.call-done = bf16[4096,512]{0,1:T(8,128)(2,1)} async-done(((bf16[512,512]{0,1:T(8,128)(2,1)}), bf16[4096,512]{0,1:T(8,128)(2,1)}) %all-gather.16.cloned.1.call-update) | async-done | bytes 4194320 | tf_op jit(solution)/shard_map/all_gather | solution.py:164
  193.4 4.4 copy.135
  201.3 82.8 %while.39 = (s32[]{:T(128)}, f32[4,512]{1,0:T(4,128)S(1)}, f32[4,512]{1,0:T(4,128)S(1)}, f32[4,512,64]{1,2,0:T(8,128)S(1)}, s32[8,512]{1,0:T(8,128)S(1)}, /*inde...) while((s32[]{:T(128)}, f32[4,512]{1,0:T(4,128)S(1)}, ...), condition=%wide.region_7.8_spmd.clone, body=%wide.region_4.7_spmd.clone.sunk | while | flops 289548288 | bytes 37631156 | solution.py:188
  226.6 3.7 fusion.134
  247.0 4.3 fusion.134
  268.3 3.7 fusion.134
  278.6 3.7 fusion.134
  285.0 4.5 all-to-all-start.1
  289.5 16.9 %all-gather.3 = bf16[4,1,256]{2,1,0:T(2,128)(2,1)S(1)} all-gather(bf16[1,1,256]{2,1,0:T(2,128)(2,1)S(1)} %reshape.518), channel_id=1, replica_groups=mesh['ctx'=8,'fsdp'=4] {'fsdp'}, dimensions={0}, use_global_device_ids=true | all-gather | bytes 2560 | tf_op jit(solution)/shard_map/all_gather | solution.py:109
  306.4 14.0 %all_gather.65 = bf16[4096]{0:T(1024)(128)(2,1)S(1)} all-gather(bf16[1024]{0:T(1024)(128)(2,1)S(1)} %copy-done.30), channel_id=1, replica_groups=mesh['ctx'=8,'fsdp'=4] {'fsdp'}, dimensions={0}, use_global_device_ids=true | all-gather | bytes 10240 | tf_op jit(solution)/shard_map/all_gather | solution.py:112
  320.4 8.6 all-gather.5
  329.1 10.8 all-gather.4
  342.3 54.3 %all-gather.20.cloned.1.call-done = bf16[1024,4096]{1,0:T(8,128)(2,1)} async-done(((bf16[256,4096]{1,0:T(8,128)(2,1)}), bf16[1024,4096]{1,0:T(8,128)(2,1)}) %all-gather.20.cloned.1.call-update) | async-done | bytes 8388624 | tf_op jit(solution)/shard_map/all_gather | solution.py:104
  396.6 6.1 convolution_add_fusion
  402.7 143.1 %all-gather.22.cloned.1.call-done = bf16[4096,1024]{1,0:T(8,128)(2,1)} async-done(((bf16[1024,1024]{1,0:T(8,128)(2,1)}), bf16[4096,1024]{1,0:T(8,128)(2,1)}) %all-gather.22.cloned.1.call-update) | async-done | bytes 8388624 | tf_op jit(solution)/shard_map/all_gather | solution.py:105
  545.9 8.9 fusion.91
  559.1 11.8 all_to_all.61
  572.7 9.0 all_gather.69
  581.7 7.2 convolution_convert_fusion
  591.1 9.0 all_gather.70
  600.8 86.1 %while.40 = (s32[]{:T(128)}, f32[4,512,64]{1,2,0:T(8,128)}, s32[8,512]{1,0:T(8,128)S(1)}, s32[512]{0:T(512)S(1)}, bf16[8,512,2,4,64]{1,4,3,2,0:T(8,128)(2,1)}, /...) while((s32[]{:T(128)}, f32[4,512,64]{1,2,0:T(8,128)}, ...), condition=%wide.region_14.15_spmd.clone, body=%wide.region_13.14_spmd.clone.sunk | while | flops 413270016 | bytes 14479547 | solution.py:278
  605.9 5.7 fusion.140
  616.6 6.1 fusion.140
  627.7 5.6 fusion.140
  638.3 5.6 fusion.140
  648.9 5.6 fusion.140
  659.5 5.6 fusion.140
  670.1 5.9 fusion.140
  681.0 5.9 fusion.140
  688.7 4.4 copy.136
  696.5 118.5 %while.41 = (s32[]{:T(128)}, f32[4,512,64]{1,2,0:T(8,128)}, f32[4,512,64]{1,2,0:T(8,128)}, s32[512]{0:T(512)S(1)}, s32[8,512]{1,0:T(8,128)S(1)}, /*index=5*/bf16...) while((s32[]{:T(128)}, f32[4,512,64]{1,2,0:T(8,128)}, ...), condition=%wide.region_16.17_spmd.clone, body=%wide.region_15.16_spmd.clone.sunk | while | flops 555089920 | bytes 21303980 | solution.py:335
  701.5 5.5 fusion.145
  706.9 4.2 fusion.146
  716.1 5.6 fusion.145
  721.7 4.3 fusion.146
  731.0 5.6 fusion.145
  736.6 4.3 fusion.146
  745.8 5.6 fusion.145
  751.4 4.3 fusion.146
  760.7 5.6 fusion.145
  766.2 4.3 fusion.146
  775.5 5.6 fusion.145
  781.1 4.3 fusion.146
  790.3 5.6 fusion.145
  795.9 4.3 fusion.146
  805.2 5.6 fusion.145
  810.7 4.3 fusion.146
  825.9 3.9 copy.123
  829.8 6.9 convolution_convert_fusion.1
  836.7 7.3 all-to-all-done.3
  848.0 6.6 pad_maximum_fusion
  854.8 279.0 %reduce-scatter.3.cloned.1.call-done = bf16[256,8192]{1,0:T(8,128)(2,1)} async-done(((bf16[1024,8192]{1,0:T(8,128)(2,1)}), bf16[256,8192]{1,0:T(8,128)(2,1)}) %reduce-scatter.3.cloned.1.call-update) | async-done | bytes 4194320 | tf_op jit(solution)/shard_map/reduce_scatter | solution.py:393
  1133.8 10.4 all-gather.6
  1146.8 6.4 fusion.52
  1153.7 5.2 multiply_reduce_fusion.1
  1159.0 16.3 %all-reduce.10 = (bf16[1024]{0:T(1024)(128)(2,1)S(1)}, bf16[1024]{0:T(1024)(128)(2,1)S(1)}, bf16[16,128]{1,0:T(8,128)(2,1)S(1)}, bf16[1024]{0:T(1024)(128)(2,1)S...) all-reduce(bf16[1024]{0:T(1024)(128)(2,1)S(1)} %get-tuple-element.5, ...), channel_id=2, replica_groups=mesh['ctx'=8,'fsdp'=4] {'fsdp'}, use_global_device_ids=true, to_apply=%region_20.21.clone | all-reduce | flops 12288 | bytes 49152
  1175.8 12.6 %all-reduce.8 = (bf16[256]{0:T(256)(128)(2,1)S(1)}, bf16[256]{0:T(256)(128)(2,1)S(1)}, bf16[4,128]{1,0:T(4,128)(2,1)S(1)}, bf16[256]{0:T(256)(128)(2,1)S(1)}, bf...) all-reduce(bf16[256]{0:T(256)(128)(2,1)S(1)} %dynamic-slice.1, ...), channel_id=1, replica_groups=mesh['ctx'=8,'fsdp'=4] {'ctx'}, use_global_device_ids=true, to_apply=%region_21.22 | all-reduce | flops 3072 | bytes 12288 | tf_op jit(solution)/shard_map/psum | solution.py:410
  1193.9 49.0 %all-reduce.13.cloned.1.call-done = (bf16[256,8192]{1,0:T(8,128)(2,1)}, bf16[1024,1024]{1,0:T(8,128)(2,1)}) async-done(((bf16[256,8192]{1,0:T(8,128)(2,1)}, bf16[1024,1024]{1,0:T(8,128)(2,1)}), (bf16[256,8192]{1,0:T(8,128)(2,1)}, bf16[1024,1024]{1,0:T(8,128)(2,1)})) %all-reduce.13.cloned.1.call-update) | async-done | bytes 6291472 | tf_op jit(solution)/shard_map/psum | solution.py:408
  (403 shorter events, 209.4 us)
Async XLA Ops:
  7.2 120.5 %all-gather.14.cloned.1.call-start = ((), (), s32[]{:S(2)}) async-start(), calls=%async_computation.6 | async-start | bytes 7864320 | tf_op jit(solution)/shard_map/all_gather | solution.py:102
  7.9 185.5 %all-gather.16.cloned.1.call-start = ((), (), s32[]{:S(2)}) async-start(), calls=%async_computation.7 | async-start | bytes 4718592 | tf_op jit(solution)/shard_map/all_gather | solution.py:164
  21.2 25.1 %copy-start.18 = (f32[4,1,256]{2,1,0:T(1,128)}, f32[4,1,256]{2,1,0:T(1,128)S(1)}, u32[]{:S(2)}) copy-start(f32[4,1,256]{2,1,0:T(1,128)S(1)} %convert_element_type.263) | copy-start | bytes 12292
  29.7 16.6 %copy-start.16 = (f32[4,1,256]{2,1,0:T(1,128)}, f32[4,1,256]{2,1,0:T(1,128)S(1)}, u32[]{:S(2)}) copy-start(f32[4,1,256]{2,1,0:T(1,128)S(1)} %convert_element_type.262) | copy-start | bytes 12292
  30.8 1.4 copy-start.20
  30.9 15.5 %copy-start.24 = (f32[128]{0:T(128)}, f32[128]{0:T(128)S(1)}, u32[]{:S(2)}) copy-start(f32[128]{0:T(128)S(1)} %div.129) | copy-start | bytes 1540
  32.1 13.0 %copy-start.28 = (f32[2,64]{1,0:T(2,128)}, f32[2,64]{1,0:T(2,128)S(1)}, u32[]{:S(2)}) copy-start(f32[2,64]{1,0:T(2,128)S(1)} %add_rsqrt_fusion) | copy-start | bytes 1540
  32.2 14.2 %copy-start.26 = (f32[128]{0:T(128)}, f32[128]{0:T(128)S(1)}, u32[]{:S(2)}) copy-start(f32[128]{0:T(128)S(1)} %rsqrt.21) | copy-start | bytes 1540
  155.5 3.2 copy-start.31
  155.5 3.7 copy-start.32
  156.7 183.1 %all-gather.18.cloned.1.call-start = ((), (), s32[]{:S(2)}) async-start(), calls=%async_computation.8 | async-start | bytes 2621440 | tf_op jit(solution)/shard_map/all_gather | solution.py:103
  157.5 239.2 %all-gather.20.cloned.1.call-start = ((), (), s32[]{:S(2)}) async-start(), calls=%async_computation.9 | async-start | bytes 10485760 | tf_op jit(solution)/shard_map/all_gather | solution.py:104
  158.0 387.8 %all-gather.22.cloned.1.call-start = ((), (), s32[]{:S(2)}) async-start(), calls=%async_computation.10 | async-start | bytes 10485760 | tf_op jit(solution)/shard_map/all_gather | solution.py:105
  201.3 88.3 %copy-start.33 = (bf16[256]{0:T(256)(128)(2,1)S(1)}, bf16[256]{0:T(256)(128)(2,1)}, u32[]{:S(2)}) copy-start(bf16[256]{0:T(256)(128)(2,1)} %param.30) | copy-start | bytes 1540
  201.3 105.1 %copy-start.30 = (bf16[1024]{0:T(1024)(128)(2,1)S(1)}, bf16[1024]{0:T(1024)(128)(2,1)}, u32[]{:S(2)}) copy-start(bf16[1024]{0:T(1024)(128)(2,1)} %param.34) | copy-start | bytes 6148
  201.3 119.2 %copy-start.34 = (bf16[256]{0:T(256)(128)(2,1)S(1)}, bf16[256]{0:T(256)(128)(2,1)}, u32[]{:S(2)}) copy-start(bf16[256]{0:T(256)(128)(2,1)} %param.32) | copy-start | bytes 1540
  201.3 127.8 %copy-start.35 = (bf16[256]{0:T(256)(128)(2,1)S(1)}, bf16[256]{0:T(256)(128)(2,1)}, u32[]{:S(2)}) copy-start(bf16[256]{0:T(256)(128)(2,1)} %param.31) | copy-start | bytes 1540
  201.3 138.6 %copy-start.4 = (bf16[1,2,1,64,1024]{4,3,2,1,0:T(8,128)(2,1)S(1)}, bf16[1,2,1,64,1024]{4,3,2,1,0:T(8,128)(2,1)}, u32[]{:S(2)}) copy-start(bf16[1,2,1,64,1024]{4,3,2,1,0:T(8,128)(2,1)} %param.22) | copy-start | bytes 786436
  206.1 3.8 copy-start
  216.3 3.8 copy-start
  226.6 3.8 copy-start
  236.8 3.8 copy-start
  247.0 4.6 copy-start
  258.1 3.8 copy-start
  268.3 3.8 copy-start
  278.6 3.8 copy-start
  284.0 118.7 %copy-start.13 = (f32[4,512,64]{1,2,0:T(8,128)}, f32[4,512,64]{1,2,0:T(8,128)S(1)}, u32[]{:S(2)}) copy-start(f32[4,512,64]{1,2,0:T(8,128)S(1)} %get-tuple-element.173) | copy-start | bytes 1572868
  285.0 54.9 %all-to-all-start.1 = ((bf16[4,128,256]{1,2,0:T(8,128)(2,1)}), bf16[4,128,256]{1,2,0:T(8,128)(2,1)S(1)}, u32[]{:S(2)}, u32[]{:S(2)}) async-start(bf16[4,128,256]{1,2,0:T(8,128)(2,1)} %copy.115), calls=%async_computation.1 | async-start | bytes 524288 | tf_op jit(solution)/shard_map/all_to_all | solution.py:199
  289.5 399.1 %all-gather.24.cloned.1.call-start = ((), (), s32[]{:S(2)}) async-start(), calls=%async_computation.11 | async-start | bytes 4718592 | tf_op jit(solution)/shard_map/all_gather | solution.py:289
  339.9 56.8 %copy-start.10 = (bf16[4,128,256]{1,2,0:T(8,128)(2,1)}, bf16[4,128,256]{1,2,0:T(8,128)(2,1)S(1)}, u32[]{:S(2)}) copy-start(bf16[4,128,256]{1,2,0:T(8,128)(2,1)S(1)} %all-to-all-done.1) | copy-start | bytes 786436
  396.6 149.2 %copy-start.8 = (bf16[1,2,1,64,1024]{4,3,2,1,0:T(8,128)(2,1)S(1)}, bf16[1,2,1,64,1024]{4,3,2,1,0:T(8,128)(2,1)}, u32[]{:S(2)}) copy-start(bf16[1,2,1,64,1024]{4,3,2,1,0:T(8,128)(2,1)} %param.37) | copy-start | bytes 786436
  545.9 8.9 copy-start.1
  554.7 3.0 copy-start.7
  554.7 3.3 copy-start.6
  557.8 13.4 %copy-start.15 = (bf16[512,1,4,64]{0,3,2,1:T(8,128)(2,1)S(1)}, bf16[512,1,4,64]{0,3,2,1:T(8,128)(2,1)}, u32[]{:S(2)}) copy-start(bf16[512,1,4,64]{0,3,2,1:T(8,128)(2,1)} %get-tuple-element.618) | copy-start | bytes 786436
  572.0 282.7 %reduce-scatter.5.cloned.1.call-start = ((), (), s32[]{:S(2)}) async-start(), calls=%async_computation.13 | async-start | bytes 10485760 | tf_op jit(solution)/shard_map/reduce_scatter | solution.py:399
  589.0 1.1 copy-start.14
  601.0 5.0 copy-start.23
  611.6 5.0 copy-start.23
  622.7 5.0 copy-start.23
  633.3 5.0 copy-start.23
  643.9 5.0 copy-start.23
  654.5 5.0 copy-start.23
  665.1 5.0 copy-start.23
  676.0 5.0 copy-start.23
  816.1 7.4 copy-start.17
  816.2 7.3 copy-start.19
  816.2 7.3 copy-start.21
  816.2 7.3 copy-start.29
  817.3 6.5 copy-start.11
  819.7 24.3 %all-to-all-start.3 = ((bf16[4,128,768]{1,2,0:T(8,128)(2,1)}), bf16[4,128,768]{1,2,0:T(8,128)(2,1)S(1)}, u32[]{:S(2)}, u32[]{:S(2)}) async-start(bf16[4,128,768]{1,2,0:T(8,128)(2,1)} %copy.122), calls=%async_computation.3 | async-start | bytes 1572864 | tf_op jit(solution)/shard_map/all_to_all | solution.py:345
  823.2 310.5 %reduce-scatter.3.cloned.1.call-start = ((), (), s32[]{:S(2)}) async-start(), calls=%async_computation.12 | async-start | bytes 20971520 | tf_op jit(solution)/shard_map/reduce_scatter | solution.py:393
  844.0 3.4 copy-start.2
  844.0 4.0 copy-start.5
  854.6 279.1 %copy-start.9 = (bf16[1,2,1,64,1024]{4,3,2,1,0:T(8,128)(2,1)S(1)}, bf16[1,2,1,64,1024]{4,3,2,1,0:T(8,128)(2,1)}, u32[]{:S(2)}) copy-start(bf16[1,2,1,64,1024]{4,3,2,1,0:T(8,128)(2,1)} %param.37) | copy-start | bytes 786436
  854.7 279.2 %copy-start.36 = (bf16[256]{0:T(256)(128)(2,1)S(1)}, bf16[256]{0:T(256)(128)(2,1)}, u32[]{:S(2)}) copy-start(bf16[256]{0:T(256)(128)(2,1)} %param.36) | copy-start | bytes 1540
  854.7 289.6 %copy-start.37 = (u32[32]{0:T(128)S(1)}, u32[32]{0:T(128)}, u32[]{:S(2)}) copy-start(u32[32]{0:T(128)} %constant.253) | copy-start | bytes 388
  854.7 388.3 %all-reduce.13.cloned.1.call-start = ((), (), s32[]{:S(2)}) async-start(), calls=%async_computation.14 | async-start | bytes 12582912 | tf_op jit(solution)/shard_map/psum | solution.py:408
  1146.8 7.0 copy-start.25
  1146.8 6.9 copy-start.27
  1153.2 5.8 copy-start.22
  1243.0 3.6 copy-start.3
  1247.6 2.5 copy-start.12
Sparse Core Ops, SparseCore 0:
  9.6 118.0 all-gather.13
  156.8 36.4 all-gather.15
  194.9 45.7 all-gather.17
  242.2 154.3 all-gather.19
  398.0 147.7 all-gather.21
  572.2 36.5 all-gather.23
  611.1 144.3 reduce-scatter.4
  854.8 278.9 reduce-scatter.2
  1137.5 105.4 all-reduce.12
where the time goes:
time: 1260 us
  waiting for transfers between devices  649 us (52%)
  matrix products  264 us (21%)
  blocking collectives  176 us (14%)
  other arithmetic  72.4 us (6%)
  local copies, waits for them, and re-layouts  71.4 us (6%)
  between operations  16.9 us (1%)
    reduce_scatter x1, waiting for transfers between devices, local(): lax.psum_scatter(jnp.concatenate([term_qkv, term_out, term_up], axis=1).a...  279 us
    all_gather x1, waiting for transfers between devices, local(): lax.all_gather(w_down, 'fsdp', axis=0, tiled=True)  143 us
    all_gather x1, waiting for transfers between devices, local(): lax.all_gather(w_qkv, 'fsdp', axis=0, tiled=True)  81.4 us
    dot_general x24, matrix products, scores_of(): jnp.einsum('qhd,khd->hqk', query_rows, key_rows, preferred_element_type=j...  70.7 us
    all_gather x1, waiting for transfers between devices, local(): lax.all_gather(w_up, 'fsdp', axis=0, tiled=True)  54.3 us
    psum x1, waiting for transfers between devices, local(): lax.psum(feature_part, 'ctx').astype(jnp.float32)  49 us
    dot_general x8, matrix products, query_key_step(): jnp.einsum('hqk,khd->hqd', grad_score, kv_rows[:, 0], preferred_element_t...  46.2 us
    dot_general x8, matrix products, query_step(): jnp.einsum('hqk,qhd->hkd', grad_score, pair_now[:, 0], preferred_element_...  44.5 us
  transfers between devices with their start and end apart: 11, of which 7 were waited for; matrix products, arithmetic and copies ran while one was open for 30% of the time, Pallas kernels for 0%

commit v1 on v0

v1 whole, which is shorter than its diff:
```python
import functools

import jax
import jax.numpy as jnp
from jax import lax
from jax.experimental import pallas as pl
from jax.experimental.pallas import tpu as pltpu
from jax.sharding import PartitionSpec as P

EPSILON = 1e-05
NEGATIVE = -1e30
TANH_SCALE = 0.7978845608028654


def gelu_tanh(values):
    return (
        0.5 * values * (1.0 + jnp.tanh(TANH_SCALE * (values + 0.044715 * values * values * values)))
    )


def norm_parts(rows_in):
    centred = rows_in - jnp.mean(rows_in, axis=-1, keepdims=True)
    inv_std = lax.rsqrt(jnp.mean(centred * centred, axis=-1, keepdims=True) + EPSILON)
    return (centred * inv_std, inv_std)


def norm_back(d_norm, gain, normed, inv_std):
    scaled = d_norm * gain
    return inv_std * (
        scaled
        - jnp.mean(scaled, axis=-1, keepdims=True)
        - normed * jnp.mean(scaled * normed, axis=-1, keepdims=True)
    )


TILE_BLOCKS = 4


def dot_nt(left, right):
    return lax.dot_general(left, right, (((1,), (1,)), ((), ())), preferred_element_type=jnp.float32)


def dot_nn(left, right):
    return jnp.dot(left, right, preferred_element_type=jnp.float32)


def query_places(tile, part, query_rows, tile_rows, block_span):
    lane = lax.broadcasted_iota(jnp.int32, (1, tile_rows), 1)
    block = tile * TILE_BLOCKS + lane // query_rows
    return (block * block_span + part * query_rows + lane % query_rows).astype(jnp.float32)


def key_places(block, block_span):
    row = lax.broadcasted_iota(jnp.int32, (block_span, 1), 0)
    return (block * block_span + row).astype(jnp.float32)


def sort_rows(slots, source, first, half, width, target, scale):
    blocks = source.shape[0]

    def step(block, carry):
        packed = source[slots[block], pl.ds(first, half), :].astype(jnp.float32) * scale
        base = pl.multiple_of(block * 2 * half, 2 * half)
        target[pl.ds(base, half), :] = packed[:, :width].astype(target.dtype)
        target[pl.ds(base + half, half), :] = packed[:, width:].astype(target.dtype)
        return carry

    lax.fori_loop(0, blocks, step, 0)


def unsort_rows(slots, source, first, half, target):
    blocks = target.shape[0]

    def step(block, carry):
        base = pl.multiple_of(block * 2 * half, 2 * half)
        packed = jnp.concatenate(
            [source[pl.ds(base, half), :], source[pl.ds(base + half, half), :]], axis=1
        )
        target[slots[block], pl.ds(first, half), :] = packed.astype(target.dtype)
        return carry

    lax.fori_loop(0, blocks, step, 0)


def attend_kernel(
    block_span, slots, part, slope, packed, out, out_t, lse, sorted_q, run_max, run_sum, sorted_o
):
    blocks = packed.shape[0]
    half = packed.shape[1] - block_span
    width = packed.shape[2] // 2
    rows = 2 * half
    tile_rows = TILE_BLOCKS * rows
    sort_rows(slots, packed, block_span, half, width, sorted_q, 0.125)
    run_max[...] = jnp.full_like(run_max, NEGATIVE)
    run_sum[...] = jnp.zeros_like(run_sum)
    out_t[...] = jnp.zeros_like(out_t)
    slope_now = slope[0]
    part_now = part[0]

    def key_step(block, carry):
        keys = packed[slots[block], pl.ds(0, block_span), :]
        values_t = keys[:, width:].astype(jnp.float32).T.astype(jnp.bfloat16)
        keys = keys[:, :width]
        key_pos = key_places(block, block_span)

        def tile_step(tile, inner):
            base = pl.multiple_of(tile * tile_rows, tile_rows)
            where = pl.ds(base, tile_rows)
            gap = query_places(tile, part_now, rows, tile_rows, block_span) - key_pos
            score = dot_nt(keys, sorted_q[where, :]) - slope_now * gap
            score = jnp.where(gap >= 0.0, score, NEGATIVE)
            old_max = run_max[:, where]
            new_max = jnp.maximum(old_max, jnp.max(score, axis=0, keepdims=True))
            weights = jnp.exp(score - new_max)
            shrink = jnp.exp(old_max - new_max)
            run_max[:, where] = new_max
            run_sum[:, where] = run_sum[:, where] * shrink + jnp.sum(
                weights, axis=0, keepdims=True
            )
            out_t[:, where] = out_t[:, where] * shrink + dot_nn(
                values_t, weights.astype(jnp.bfloat16)
            )
            return inner

        lax.fori_loop(block // TILE_BLOCKS, blocks // TILE_BLOCKS, tile_step, 0)
        return carry

    lax.fori_loop(0, blocks, key_step, 0)
    out_t[...] = out_t[...] / run_sum[...]
    lse[...] = run_max[...] + jnp.log(run_sum[...])
    sorted_o[...] = out_t[...].T
    unsort_rows(slots, sorted_o, 0, half, out)


def attend_back_kernel(
    block_span,
    slots,
    part,
    slope,
    packed,
    grad_out,
    out_t,
    lse,
    grads,
    sorted_q,
    sorted_g,
    delta,
    grad_q_t,
    sorted_dq,
):
    blocks = packed.shape[0]
    half = packed.shape[1] - block_span
    width = packed.shape[2] // 2
    rows = 2 * half
    tile_rows = TILE_BLOCKS * rows
    sort_rows(slots, packed, block_span, half, width, sorted_q, 0.125)
    sort_rows(slots, grad_out, 0, half, width, sorted_g, 1.0)
    delta[...] = jnp.sum(
        sorted_g[...].astype(jnp.float32).T * out_t[...], axis=0, keepdims=True
    )
    grad_q_t[...] = jnp.zeros_like(grad_q_t)
    slope_now = slope[0]
    part_now = part[0]

    def key_step(block, carry):
        keys = packed[slots[block], pl.ds(0, block_span), :]
        values = keys[:, width:]
        keys = keys[:, :width]
        keys_t = keys.astype(jnp.float32).T.astype(jnp.bfloat16)
        key_pos = key_places(block, block_span)

        def tile_step(tile, sums):
            grad_k, grad_v = sums
            base = pl.multiple_of(tile * tile_rows, tile_rows)
            where = pl.ds(base, tile_rows)
            query_now = sorted_q[where, :]
            grad_now = sorted_g[where, :]
            gap = query_places(tile, part_now, rows, tile_rows, block_span) - key_pos
            score = dot_nt(keys, query_now) - slope_now * gap
            score = jnp.where(gap >= 0.0, score, NEGATIVE)
            probs = jnp.exp(score - lse[:, where])
            grad_v = grad_v + dot_nn(probs.astype(jnp.bfloat16), grad_now)
            grad_score = probs * (dot_nt(values, grad_now) - delta[:, where])
            grad_score = grad_score.astype(jnp.bfloat16)
            grad_k = grad_k + dot_nn(grad_score, query_now)
            grad_q_t[:, where] = grad_q_t[:, where] + dot_nn(keys_t, grad_score)
            return (grad_k, grad_v)

        zero = jnp.zeros((block_span, width), jnp.float32)
        grad_k, grad_v = lax.fori_loop(
            block // TILE_BLOCKS, blocks // TILE_BLOCKS, tile_step, (zero, zero)
        )
        grads[slots[block], pl.ds(0, block_span), :] = jnp.concatenate(
            [grad_k, grad_v], axis=1
        ).astype(grads.dtype)
        return carry

    lax.fori_loop(0, blocks, key_step, 0)
    sorted_dq[...] = grad_q_t[...].T * 0.125
    unsort_rows(slots, sorted_dq, block_span, half, grads)


def smem():
    return pl.BlockSpec(memory_space=pltpu.SMEM)


def vmem():
    return pl.BlockSpec(memory_space=pltpu.VMEM)


def attend(slots, part, slope, packed, block_span):
    blocks, packed_rows, lanes = packed.shape
    half = packed_rows - block_span
    width = lanes // 2
    total = blocks * 2 * half
    return pl.pallas_call(
        functools.partial(attend_kernel, block_span),
        out_shape=(
            jax.ShapeDtypeStruct((blocks, half, lanes), jnp.bfloat16),
            jax.ShapeDtypeStruct((width, total), jnp.float32),
            jax.ShapeDtypeStruct((1, total), jnp.float32),
        ),
        in_specs=[smem(), smem(), smem(), vmem()],
        out_specs=(vmem(), vmem(), vmem()),
        scratch_shapes=[
            pltpu.VMEM((total, width), jnp.bfloat16),
            pltpu.VMEM((1, total), jnp.float32),
            pltpu.VMEM((1, total), jnp.float32),
            pltpu.VMEM((total, width), jnp.float32),
        ],
        compiler_params=pltpu.CompilerParams(vmem_limit_bytes=48 * 1024 * 1024),
        cost_estimate=pl.CostEstimate(
            flops=2 * total * blocks * block_span * lanes,
            bytes_accessed=4 * packed.size,
            transcendentals=total * blocks * block_span // 2,
        ),
        name="attend",
    )(slots, part, slope, packed)


def attend_back(slots, part, slope, packed, grad_out, out_t, lse, block_span):
    blocks, packed_rows, lanes = packed.shape
    half = packed_rows - block_span
    width = lanes // 2
    total = blocks * 2 * half
    return pl.pallas_call(
        functools.partial(attend_back_kernel, block_span),
        out_shape=jax.ShapeDtypeStruct(packed.shape, jnp.bfloat16),
        in_specs=[smem(), smem(), smem(), vmem(), vmem(), vmem(), vmem()],
        out_specs=vmem(),
        scratch_shapes=[
            pltpu.VMEM((total, width), jnp.bfloat16),
            pltpu.VMEM((total, width), jnp.bfloat16),
            pltpu.VMEM((1, total), jnp.float32),
            pltpu.VMEM((width, total), jnp.float32),
            pltpu.VMEM((total, width), jnp.float32),
        ],
        compiler_params=pltpu.CompilerParams(vmem_limit_bytes=48 * 1024 * 1024),
        cost_estimate=pl.CostEstimate(
            flops=5 * total * blocks * block_span * width,
            bytes_accessed=8 * packed.size,
            transcendentals=total * blocks * block_span // 2,
        ),
        name="attend_back",
    )(slots, part, slope, packed, grad_out, out_t, lse)


def local(
    hidden,
    block_order,
    alibi_slopes,
    ln1_gain,
    ln1_bias,
    w_qkv,
    qv_bias,
    w_out,
    out_bias,
    ln2_gain,
    ln2_bias,
    w_up,
    up_bias,
    w_down,
    down_bias,
    d_output,
):
    f32 = jnp.float32
    b16 = jnp.bfloat16
    half_rows = hidden.shape[3]
    width = hidden.shape[4]
    tok_rows = 2 * half_rows
    groups = lax.axis_size("fsdp")
    ctx_size = lax.axis_size("ctx")
    head_count = alibi_slopes.shape[0]
    head_width = width // head_count
    heads = head_count // groups
    span = tok_rows * groups
    block_span = half_rows * groups
    parts = ctx_size // heads
    part_groups = groups // parts
    query_rows = part_groups * half_rows
    half = query_rows // 2
    qkv_cols = 3 * width // groups
    up_cols = w_up.shape[1] // groups
    ctx_index = lax.axis_index("ctx")
    group_index = lax.axis_index("fsdp")
    shard = width // groups

    def gather(rows, axis_name):
        return lax.all_gather(rows, axis_name, axis=0, tiled=True)

    def exchange(rows, axis_name):
        return lax.all_to_all(rows, axis_name, split_axis=0, concat_axis=0, tiled=True)

    def scatter(rows):
        return lax.psum_scatter(
            rows.astype(b16), "fsdp", scatter_dimension=0, tiled=True
        ).astype(f32)

    cut = w_qkv.shape[0] // ctx_size
    cut_qkv = lax.dynamic_slice_in_dim(w_qkv, ctx_index * cut, cut).reshape(cut, groups, qkv_cols)
    cut_up = lax.dynamic_slice_in_dim(w_up, ctx_index * cut, cut).reshape(cut, groups, up_cols)
    cut_both = exchange(
        jnp.concatenate([cut_qkv, cut_up], axis=2).transpose(1, 0, 2), "fsdp"
    )

    def own_columns(cut_cols):
        whole = lax.all_gather(cut_cols, "ctx", axis=0)
        return whole.transpose(1, 0, 2, 3).reshape(width, cut_cols.shape[2])

    own_qkv = own_columns(cut_both[:, :, :qkv_cols])
    own_up = own_columns(cut_both[:, :, qkv_cols:])

    own_rows = hidden.reshape(tok_rows, width)
    grad_out = d_output.reshape(tok_rows, width)
    small = jnp.stack([ln1_gain, ln1_bias, out_bias, ln2_gain, ln2_bias, down_bias])
    small = jnp.pad(small, ((0, 10), (0, width - shard)))
    with_small = gather(jnp.concatenate([own_rows, small], axis=0), "fsdp").reshape(
        groups, tok_rows + 16, width
    )
    full_small = (
        with_small[:, tok_rows : tok_rows + 6, :shard].transpose(1, 0, 2).reshape(6, width)
    ).astype(f32)
    full_g1, full_b1, full_bo, full_g2, full_b2, full_bd = (full_small[i] for i in range(6))
    all_rows = with_small[:, :tok_rows].reshape(span, width)
    all_grad = gather(grad_out, "fsdp")

    rows_in = own_rows.astype(f32)
    normed_one, inv_one = norm_parts(rows_in)
    first_in = (norm_parts(all_rows.astype(f32))[0] * full_g1 + full_b1).astype(b16)
    joined_bias = jnp.concatenate(
        [
            qv_bias[:, :head_width],
            jnp.zeros((heads, head_width), b16),
            qv_bias[:, head_width:],
        ],
        axis=1,
    ).reshape(qkv_cols)
    joined = (dot_nn(first_in, own_qkv) + joined_bias.astype(f32)).astype(b16)

    joined = joined.reshape(parts, part_groups, 2, half_rows, heads, 3 * head_width)

    def pack_queries(rows):
        rows = rows.transpose(4, 0, 2, 1, 3, 5).reshape(
            ctx_size, 2, 2, half, head_width
        )
        return jnp.concatenate([rows[:, :, 0], rows[:, :, 1]], axis=-1)

    def unpack_queries(rows):
        rows = jnp.stack([rows[..., :head_width], rows[..., head_width:]], axis=2)
        return rows.reshape(
            heads, parts, 2, part_groups, half_rows, head_width
        ).transpose(1, 3, 2, 4, 0, 5)

    keys_values = (
        joined[..., head_width:]
        .transpose(4, 2, 0, 1, 3, 5)
        .reshape(heads, 1, 2, block_span, 2 * head_width)
    )
    keys_values = jnp.broadcast_to(
        keys_values, (heads, parts, 2, block_span, 2 * head_width)
    ).reshape(ctx_size, 2, block_span, 2 * head_width)
    packed = exchange(
        jnp.concatenate([keys_values, pack_queries(joined[..., :head_width])], axis=2), "ctx"
    ).reshape(2 * ctx_size, block_span + half, 2 * head_width)

    flat_order = block_order.reshape(-1)
    slot_ids = jnp.arange(2 * ctx_size, dtype=jnp.int32)
    slots = jnp.sum(
        jnp.where(flat_order[None, :] == slot_ids[:, None], slot_ids[None, :], 0), axis=1
    ).astype(jnp.int32)
    part = (ctx_index % parts).astype(jnp.int32).reshape(1)
    slope = lax.dynamic_slice_in_dim(alibi_slopes, group_index * heads + ctx_index // parts, 1)
    out_packed, out_t, lse = attend(slots, part, slope, packed, block_span)

    attended = unpack_queries(
        exchange(out_packed.reshape(ctx_size, 2, half, 2 * head_width), "ctx")
    ).reshape(span, heads * head_width)
    middle = rows_in + scatter(dot_nn(attended, w_out)) + full_bo
    normed_two, inv_two = norm_parts(middle)
    second_in = gather((normed_two * full_g2 + full_b2).astype(b16), "fsdp")
    hidden_pre = dot_nn(second_in, own_up) + up_bias.astype(f32)
    activated, gelu_pull = jax.vjp(gelu_tanh, hidden_pre)
    activated = activated.astype(b16)
    result = middle + scatter(dot_nn(activated, w_down)) + full_bd
    output = result.astype(b16).reshape(hidden.shape)

    grad_act = dot_nt(all_grad, w_down).astype(b16)
    grad_pre = gelu_pull(grad_act.astype(f32))[0].astype(b16)
    grad_second = scatter(dot_nt(grad_pre, own_up))
    grad_middle = grad_out.astype(f32) + norm_back(grad_second, full_g2, normed_two, inv_two)
    grad_branch = gather(grad_middle.astype(b16), "fsdp")
    grad_attended = dot_nt(grad_branch, w_out).astype(b16)
    grad_packed = exchange(
        pack_queries(
            grad_attended.reshape(parts, part_groups, 2, half_rows, heads, head_width)
        ),
        "ctx",
    ).reshape(2 * ctx_size, half, 2 * head_width)
    grads = attend_back(slots, part, slope, packed, grad_packed, out_t, lse, block_span)
    grads = exchange(
        grads.reshape(ctx_size, 2, block_span + half, 2 * head_width), "ctx"
    )
    grad_q = unpack_queries(grads[:, :, block_span:]).reshape(span, heads, head_width)
    grad_kv = jnp.sum(
        grads[:, :, :block_span]
        .reshape(heads, parts, 2, groups, half_rows, 2 * head_width)
        .astype(f32),
        axis=1,
    ).astype(b16)
    grad_kv = grad_kv.transpose(2, 1, 3, 0, 4).reshape(span, heads, 2 * head_width)
    grad_joined = jnp.concatenate([grad_q, grad_kv], axis=2).reshape(span, qkv_cols)
    grad_first = scatter(dot_nt(grad_joined, own_qkv))
    grad_rows = grad_middle + norm_back(grad_first, full_g1, normed_one, inv_one)
    d_hidden = grad_rows.astype(b16).reshape(hidden.shape)

    def dot_tn(left, right):
        return lax.dot_general(
            left, right, (((0,), (0,)), ((), ())), preferred_element_type=f32
        ).astype(b16)

    def own_row_sums(cols):
        cols = cols.reshape(groups, ctx_size, cut, cols.shape[1]).transpose(1, 0, 2, 3)
        summed = lax.psum_scatter(cols, "ctx", scatter_dimension=0, tiled=True)
        moved = exchange(summed[0], "fsdp").transpose(1, 0, 2)
        return gather(moved.reshape(cut, -1), "ctx").astype(f32)

    d_w_down, d_w_out = lax.psum(
        (dot_tn(activated, all_grad), dot_tn(attended, grad_branch)), "ctx"
    )
    d_w_up = own_row_sums(dot_tn(second_in, grad_pre))
    d_w_qkv = own_row_sums(dot_tn(first_in, grad_joined))

    def own_sum(rows):
        return lax.dynamic_slice_in_dim(
            jnp.sum(rows.astype(f32), axis=0), group_index * shard, shard
        )

    joined_sums = jnp.sum(grad_joined.astype(f32), axis=0).reshape(heads, 3, head_width)
    sum_qv = jnp.concatenate([joined_sums[:, 0], joined_sums[:, 2]], axis=1)
    early = lax.psum(
        jnp.concatenate(
            [
                jnp.sum(grad_pre.astype(f32), axis=0),
                own_sum(grad_branch),
                own_sum(all_grad),
            ]
        ),
        "ctx",
    )
    d_up_bias = early[:up_cols]
    d_out_bias = early[up_cols : up_cols + shard]
    d_down_bias = early[up_cols + shard :]
    spread = jnp.where(
        jnp.arange(groups)[:, None] == group_index, sum_qv.reshape(1, -1), 0.0
    ).reshape(-1)
    late = lax.psum(
        jnp.concatenate(
            [
                jnp.sum(grad_first * normed_one, axis=0),
                jnp.sum(grad_first, axis=0),
                jnp.sum(grad_second * normed_two, axis=0),
                jnp.sum(grad_second, axis=0),
                spread,
            ]
        ),
        ("ctx", "fsdp"),
    )
    norm_sums = late[: 4 * width].reshape(4, groups, shard)
    norm_sums = lax.dynamic_slice_in_dim(norm_sums, group_index, 1, axis=1)[:, 0]
    d_qv_bias = lax.dynamic_slice_in_dim(
        late[4 * width :].reshape((groups,) + sum_qv.shape), group_index, 1
    )[0]
    return (
        output,
        d_hidden,
        norm_sums[0],
        norm_sums[1],
        d_w_qkv,
        d_qv_bias,
        d_w_out.astype(f32),
        d_out_bias,
        norm_sums[2],
        norm_sums[3],
        d_w_up,
        d_up_bias,
        d_w_down.astype(f32),
        d_down_bias,
    )


def solution(mesh):
    placed = (
        P("ctx", None, "fsdp", None, None),
        P(),
        P(),
        P("fsdp"),
        P("fsdp"),
        P("fsdp", None),
        P("fsdp", None),
        P("fsdp", None),
        P("fsdp"),
        P("fsdp"),
        P("fsdp"),
        P("fsdp", None),
        P("fsdp"),
        P("fsdp", None),
        P("fsdp"),
        P("ctx", None, "fsdp", None, None),
    )
    return jax.shard_map(
        local,
        mesh=mesh,
        in_specs=placed,
        out_specs=(
            P("ctx", None, "fsdp", None, None),
            P("ctx", None, "fsdp", None, None),
            P("fsdp"),
            P("fsdp"),
            P("fsdp", None),
            P("fsdp", None),
            P("fsdp", None),
            P("fsdp"),
            P("fsdp"),
            P("fsdp"),
            P("fsdp", None),
            P("fsdp"),
            P("fsdp", None),
            P("fsdp"),
        ),
        check_vma=False,
    )
```

time: 1260 us -> 662 us (0.53)
  waiting for transfers between devices: 649 us -> 331 us
  matrix products: 264 us -> 37.1 us
  Pallas kernels: 0 us -> 62.7 us
  blocking collectives: 176 us -> 132 us
  other arithmetic: 72.4 us -> 37.3 us
  local copies, waits for them, and re-layouts: 71.4 us -> 37.6 us
    dot_general x68 -> x12, matrix products: 264 us -> 37.1 us  [the longest x4 13 us: dot_nn(): return jnp.dot(left, right, preferred_element_type=jnp.float32)]
    reduce_scatter x2 -> x4, waiting for transfers between devices: 279 us -> 74.4 us  [scatter(): lax.psum_scatter(rows.astype(b16), 'fsdp', scatter_dimension=0, tiled=True)]
    all_gather x6 -> x8, waiting for transfers between devices: 312 us -> 132 us  [the longest x6 84.4 us: gather(): return lax.all_gather(rows, axis_name, axis=0, tiled=True)]
    all_gather x10 -> x0, blocking collectives: 112 us -> none  [the longest x1 16.9 us: local(): lax.all_gather(out_bias, 'fsdp', axis=0, tiled=True)]
    unnamed x9 -> x14, waiting for transfers between devices: 2.03 us -> 98.2 us
    pallas_call x0 -> x2, Pallas kernels: none -> 62.7 us  [the longest x1 36.8 us: attend_back(): pl.pallas_call(functools.partial(attend_back_kernel, block_span), out_sha...]
    psum x1 -> x0, waiting for transfers between devices: 49 us -> none  [local(): lax.psum(feature_part, 'ctx').astype(jnp.float32)]
    all_to_all x2 -> x5, blocking collectives: 34.8 us -> 82.1 us  [exchange(): lax.all_to_all(rows, axis_name, split_axis=0, concat_axis=0, tiled=True)]
  transfers between devices with their start and end apart: 11 -> 15, of which waited for: 7 -> 12; matrix products, arithmetic and copies ran while one was open for 30% -> 9% of each run, Pallas kernels for 0% -> 0%
where the time goes in v1:
time: 662 us; the launch traced here: 661 us
  waiting for transfers between devices  331 us (50%)
  blocking collectives  132 us (20%)
  Pallas kernels  62.7 us (9%)
  local copies, waits for them, and re-layouts  37.6 us (6%)
  other arithmetic  37.3 us (6%)
  matrix products  37.1 us (6%)
  between operations  14.5 us (2%)
  starting transfers between devices  8.21 us (1%)
    unnamed x14, waiting for transfers between devices  98.2 us
    all_gather x6, waiting for transfers between devices, gather(): return lax.all_gather(rows, axis_name, axis=0, tiled=True)  84.4 us
    all_to_all x5, blocking collectives, exchange(): lax.all_to_all(rows, axis_name, split_axis=0, concat_axis=0, tiled=True)  82.1 us
    reduce_scatter x4, waiting for transfers between devices, scatter(): lax.psum_scatter(rows.astype(b16), 'fsdp', scatter_dimension=0, tiled=True)  74.4 us
    all_gather x2, waiting for transfers between devices, own_columns(): whole = lax.all_gather(cut_cols, 'ctx', axis=0)  47.4 us
    psum x1, blocking collectives, local(): lax.psum(jnp.concatenate([jnp.sum(grad_first * normed_one, axis=0), jnp.s...  37.9 us
    pallas_call x1, Pallas kernels, attend_back(): pl.pallas_call(functools.partial(attend_back_kernel, block_span), out_sha...  36.8 us
    all_to_all x2, waiting for transfers between devices, exchange(): lax.all_to_all(rows, axis_name, split_axis=0, concat_axis=0, tiled=True)  26.8 us
  transfers between devices with their start and end apart: 15, of which 12 were waited for; matrix products, arithmetic and copies ran while one was open for 9% of the time, Pallas kernels for 0%

profile of v1, /device:TPU:0, one launch (start us, length us, event | category | flops | bytes accessed | tf_op | source)
XLA Modules:
  0.0 661.0 jit_solution(8486473904418689057)
XLA Ops:
  11.4 1.7 fusion.38
  15.7 30.4 %all_to_all.35 = bf16[4,32,1792]{2,1,0:T(8,128)(2,1)S(1)} all-to-all(bf16[4,32,1792]{2,1,0:T(8,128)(2,1)S(1)} %copy.114), channel_id=1, replica_groups=mesh['ctx'=8,'fsdp'=4] {'fsdp'}, dimensions={0} | all-to-all | bytes 917504 | tf_op jit(solution)/shard_map/all_to_all | solution.py:312
  47.8 6.4 all-gather.11.cloned.1.call-done
  54.2 1.5 convert_reduce_fusion
  55.7 1.6 fusion.2
  57.9 23.6 %all-gather.23.cloned.1.call-done = bf16[32,32,768]{2,1,0:T(8,128)(2,1)} async-done(((bf16[4,32,768]{2,1,0:T(8,128)(2,1)}), bf16[32,32,768]{2,1,0:T(8,128)(2,1)}) %all-gather.23.cloned.1.call-update) | async-done | bytes 1572880 | tf_op jit(solution)/shard_map/all_gather | solution.py:327
  81.5 1.5 copy.115
  83.0 1.1 copy-done.11
  84.2 1.9 add_convert_fusion
  86.0 2.7 reshape.329
  89.8 1.3 maximum_maximum_fusion
  91.1 3.6 all-to-all-start.1
  95.6 17.2 %all-to-all-done.1 = bf16[8,2,320,128]{3,2,1,0:T(8,128)(2,1)S(1)} async-done(((bf16[8,2,320,128]{3,2,1,0:T(8,128)(2,1)}), bf16[8,2,320,128]{3,2,1,0:T(8,128)(2,1)S(1)}, u32[]{:S(2)}, u32[]{:S(2)}) %all-to-all-start.1) | async-done | bytes 1310752 | tf_op jit(solution)/shard_map/all_to_all | solution.py:312
  112.8 25.9 %attend.1 = (bf16[16,64,128]{2,1,0:T(8,128)(2,1)S(1)}, f32[64,2048]{1,0:T(8,128)S(1)}, f32[1,2048]{1,0:T(1,128)S(1)}) custom-call(s32[16]{0:T(128)S(1)} %select_reduce_fusion.slots, s32[1]{0:T(128)} %bitcast.1.part, f32[1]{0:T(128)} %dynamic_slice.21.slope, bf16[16,320,128]{2,1,0:T(8,128)(2,1)S(1)} %bitcast.143), custom_call_target="tpu_custom_call" | custom-call | flops 2147483648 | bytes 2621440 | tf_op jit(solution)/shard_map/attend/pallas_call | solution.py:216
  138.7 9.3 %all_to_all.36 = bf16[8,2,64,128]{3,2,1,0:T(8,128)(2,1)S(1)} all-to-all(bf16[8,2,64,128]{3,2,1,0:T(8,128)(2,1)S(1)} %bitcast.146), channel_id=1, replica_groups=mesh['ctx'=8,'fsdp'=4] {'ctx'}, dimensions={0} | all-to-all | bytes 524288 | tf_op jit(solution)/shard_map/all_to_all | solution.py:312
  148.3 1.2 copy.118
  149.5 2.2 reshape.334
  151.7 2.5 convolution_convert_fusion.7
  154.3 1.7 slice.185
  156.0 24.6 %reduce-scatter.11.cloned.1.call-done = bf16[128,1024]{1,0:T(8,128)(2,1)} async-done(((bf16[512,1024]{1,0:T(8,128)(2,1)}), bf16[128,1024]{1,0:T(8,128)(2,1)}) %reduce-scatter.11.cloned.1.call-update) | async-done | bytes 262160 | tf_op jit(solution)/shard_map/reduce_scatter | solution.py:315
  180.7 1.2 fusion.39
  181.9 1.2 multiply_reduce_fusion
  183.1 1.9 add_convert_fusion.2
  185.9 23.9 %all-gather.25.cloned.1.call-done = bf16[32,32,1024]{2,1,0:T(8,128)(2,1)} async-done(((bf16[4,32,1024]{2,1,0:T(8,128)(2,1)}), bf16[32,32,1024]{2,1,0:T(8,128)(2,1)}) %all-gather.25.cloned.1.call-update) | async-done | bytes 2097168 | tf_op jit(solution)/shard_map/all_gather | solution.py:327
  209.7 3.2 copy.119
  212.9 26.8 %all-gather.13.cloned.1.call-done = bf16[512,1024]{1,0:T(8,128)(2,1)} async-done(((bf16[128,1024]{1,0:T(8,128)(2,1)}), bf16[512,1024]{1,0:T(8,128)(2,1)}) %all-gather.13.cloned.1.call-update) | async-done | bytes 1048592 | tf_op jit(solution)/shard_map/all_gather | solution.py:309
  239.7 4.5 fusion.48
  244.2 24.5 %all-gather.15.cloned.1.call-done = bf16[512,1024]{1,0:T(8,128)(2,1)} async-done(((bf16[128,1024]{1,0:T(8,128)(2,1)}), bf16[512,1024]{1,0:T(8,128)(2,1)}) %all-gather.15.cloned.1.call-update) | async-done | bytes 1048592 | tf_op jit(solution)/shard_map/all_gather | solution.py:309
  268.7 4.9 convert_reduce_fusion.3
  274.6 2.3 convolution_convert_fusion.4
  276.9 4.1 convolution_convert_fusion.6
  281.1 22.6 %reduce-scatter.15.cloned.1.call-done = bf16[128,1024]{1,0:T(8,128)(2,1)} async-done(((bf16[512,1024]{1,0:T(8,128)(2,1)}), bf16[128,1024]{1,0:T(8,128)(2,1)}) %reduce-scatter.15.cloned.1.call-update) | async-done | bytes 262160 | tf_op jit(solution)/shard_map/reduce_scatter | solution.py:315
  303.7 1.5 fusion.36
  305.2 27.2 %reduce-scatter.13.cloned.1.call-done = bf16[128,1024]{1,0:T(8,128)(2,1)} async-done(((bf16[512,1024]{1,0:T(8,128)(2,1)}), bf16[128,1024]{1,0:T(8,128)(2,1)}) %reduce-scatter.13.cloned.1.call-update) | async-done | bytes 262160 | tf_op jit(solution)/shard_map/reduce_scatter | solution.py:315
  332.4 2.6 fusion.40
  335.0 26.8 %all-gather.17.cloned.1.call-done = bf16[512,1024]{1,0:T(8,128)(2,1)} async-done(((bf16[128,1024]{1,0:T(8,128)(2,1)}), bf16[512,1024]{1,0:T(8,128)(2,1)}) %all-gather.17.cloned.1.call-update) | async-done | bytes 1048592 | tf_op jit(solution)/shard_map/all_gather | solution.py:309
  361.7 1.7 convolution_convert_fusion.9
  364.0 10.4 %all_to_all.37 = bf16[8,2,64,128]{3,2,1,0:T(8,128)(2,1)S(1)} all-to-all(bf16[8,2,64,128]{3,2,1,0:T(8,128)(2,1)S(1)} %pad_maximum_fusion.1), channel_id=1, replica_groups=mesh['ctx'=8,'fsdp'=4] {'ctx'}, dimensions={0} | all-to-all | bytes 524288 | tf_op jit(solution)/shard_map/all_to_all | solution.py:312
  374.4 36.8 %attend_back.1 = bf16[16,320,128]{2,1,0:T(8,128)(2,1)} custom-call(s32[16]{0:T(128)S(1)} %select_reduce_fusion.slots, s32[1]{0:T(128)} %bitcast.1.part, f32[1]{0:T(128)} %dynamic_slice.21.slope, bf16[16,320,128]{2,1,0:T(8,128)(2,1)S(1)} %bitcast.144, bf16[16,64,128]{2,1,0:T(8,128)(2,1)S(1)} %bitcast.145, f32[64,2048]{1,0:T(8,128)S(1)} %copy-done.3, ...), custom_call_target="tpu_custom_call" | custom-call | flops 2684354560 | bytes 5242880 | tf_op jit(solution)/shard_map/attend_back/pallas_call | solution.py:246
  411.2 3.7 all-to-all-start.4
  415.3 4.0 convolution_convert_fusion.1
  419.3 3.0 convolution_convert_fusion
  422.2 1.3 convolution_convert_fusion.8
  423.5 9.6 %all-to-all-done.4 = bf16[8,2,320,128]{3,2,1,0:T(8,128)(2,1)S(1)} async-done(((bf16[8,2,320,128]{3,2,1,0:T(8,128)(2,1)}), bf16[8,2,320,128]{3,2,1,0:T(8,128)(2,1)S(1)}, u32[]{:S(2)}, u32[]{:S(2)}) %all-to-all-start.4) | async-done | bytes 1310752 | tf_op jit(solution)/shard_map/all_to_all | solution.py:312
  434.1 2.4 reduce_sum.192
  436.6 1.1 copy.122
  438.4 1.2 copy.124
  439.7 3.7 convolution_convert_fusion.2
  443.4 1.0 copy-done.14
  444.5 3.4 convolution_convert_fusion.3
  448.6 97.4 %all-reduce.6.cloned.1.call-done = (bf16[8,4,32,768]{3,2,0,1:T(8,128)(2,1)}, bf16[256,1024]{1,0:T(8,128)(2,1)}, bf16[8,4,32,1024]{3,2,0,1:T(8,128)(2,1)}, bf16[1024,1024]{1,0:T(8,128)(2,1)}) async-done(((bf16[8,4,32,768]{3,2,0,1:T(8,128)(2,1)}, bf16[256,1024]{1,0:T(8,128)(2,1)}, bf16[8,4,32,1024]{3,2,0,1:T(8,128)(2,1)}, bf16[1024,1024]{1,0:T(8,128)(2,1)}), (bf16[8,4,32,768]{3,2,0,1:T(8,128)(2,1)}, ...) | async-done | bytes 6291472
  546.0 1.6 dynamic-slice_bitcast_fusion.1
  547.6 15.5 %all_to_all.38 = bf16[4,32,768]{2,1,0:T(8,128)(2,1)S(1)} all-to-all(bf16[4,32,768]{2,1,0:T(8,128)(2,1)S(1)} %dynamic-slice_bitcast_fusion.1), channel_id=1, replica_groups=mesh['ctx'=8,'fsdp'=4] {'fsdp'}, dimensions={0} | all-to-all | bytes 393216 | tf_op jit(solution)/shard_map/all_to_all | solution.py:312
  563.9 1.6 dynamic-slice_bitcast_fusion
  565.5 16.5 %all_to_all.39 = bf16[4,32,1024]{2,1,0:T(8,128)(2,1)S(1)} all-to-all(bf16[4,32,1024]{2,1,0:T(8,128)(2,1)S(1)} %dynamic-slice_bitcast_fusion), channel_id=1, replica_groups=mesh['ctx'=8,'fsdp'=4] {'fsdp'}, dimensions={0} | all-to-all | bytes 524288 | tf_op jit(solution)/shard_map/all_to_all | solution.py:312
  583.2 1.4 convert_reduce_fusion.1
  585.0 12.4 %psum.30 = f32[1536]{0:T(1024)S(1)} all-reduce(f32[1536]{0:T(1024)S(1)} %pad_maximum_fusion.2), channel_id=1, replica_groups=mesh['ctx'=8,'fsdp'=4] {'ctx'}, use_global_device_ids=true, to_apply=%region_27.28 | all-reduce | flops 1536 | bytes 12288 | tf_op jit(solution)/shard_map/psum | solution.py:460
  599.3 1.2 fusion.37
  600.6 37.9 %psum.28 = f32[6144]{0:T(1024)S(1)} all-reduce(f32[6144]{0:T(1024)S(1)} %constant_dynamic-update-slice_fusion), channel_id=1, replica_groups=mesh['ctx'=8,'fsdp'=4] {'ctx','fsdp'}, use_global_device_ids=true, to_apply=%region_21.22 | all-reduce | flops 6144 | bytes 49152 | tf_op jit(solution)/shard_map/psum | solution.py:476
  639.7 1.9 fusion.28
  641.6 1.1 convert_element_type.172
  642.7 4.1 convert_element_type.179
  646.8 3.6 convert_element_type.170
  650.3 4.1 convert_element_type.177
  (160 shorter events, 22.0 us)
Async XLA Ops:
  7.2 261.5 %copy-start = (bf16[1024,1024]{1,0:T(8,128)(2,1)S(1)}, bf16[1024,1024]{1,0:T(8,128)(2,1)}, u32[]{:S(2)}) copy-start(bf16[1024,1024]{1,0:T(8,128)(2,1)} %param.29) | copy-start | bytes 6291460
  7.2 47.0 %all-gather.11.cloned.1.call-start = ((), (), s32[]{:S(2)}) async-start(), calls=%async_computation.11 | async-start | bytes 1474560 | tf_op jit(solution)/shard_map/all_gather | solution.py:309
  13.1 68.4 %all-gather.23.cloned.1.call-start = ((), (), s32[]{:S(2)}) async-start(), calls=%async_computation.21 | async-start | bytes 1769472 | tf_op jit(solution)/shard_map/all_gather | solution.py:327
  14.2 33.5 %copy-start.17 = (bf16[4,128]{1,0:T(4,128)(2,1)S(1)}, bf16[4,128]{1,0:T(4,128)(2,1)}, u32[]{:S(2)}) copy-start(bf16[4,128]{1,0:T(4,128)(2,1)} %param.22) | copy-start | bytes 3076
  46.1 0.8 copy-start.10
  54.2 3.2 copy-start.5
  57.9 25.1 %copy-start.12 = (bf16[4,128,1024]{2,1,0:T(8,128)(2,1)}, bf16[4,128,1024]{2,1,0:T(8,128)(2,1)S(1)}, u32[]{:S(2)}) copy-start(bf16[4,128,1024]{2,1,0:T(8,128)(2,1)S(1)} %fusion.5) | copy-start | bytes 3145732
  83.0 1.1 copy-start.11
  89.8 5.0 copy-start.19
  89.8 5.1 copy-start.21
  91.1 21.7 %all-to-all-start.1 = ((bf16[8,2,320,128]{3,2,1,0:T(8,128)(2,1)}), bf16[8,2,320,128]{3,2,1,0:T(8,128)(2,1)S(1)}, u32[]{:S(2)}, u32[]{:S(2)}) async-start(bf16[8,2,320,128]{3,2,1,0:T(8,128)(2,1)} %maximum_maximum_fusion), calls=%async_computation.1 | async-start | bytes 2621440 | tf_op jit(solution)/shard_map/all_to_all | solution.py:312
  94.7 86.0 %reduce-scatter.11.cloned.1.call-start = ((), (), s32[]{:S(2)}) async-start(), calls=%async_computation.12 | async-start | bytes 1310720 | tf_op jit(solution)/shard_map/reduce_scatter | solution.py:315
  138.7 9.3 %copy-start.2 = (f32[64,2048]{1,0:T(8,128)}, f32[64,2048]{1,0:T(8,128)S(1)}, u32[]{:S(2)}) copy-start(f32[64,2048]{1,0:T(8,128)S(1)} %get-tuple-element.18.out_t) | copy-start | bytes 1572868
  154.2 31.6 %copy-start.18 = (bf16[1024]{0:T(1024)(128)(2,1)S(1)}, bf16[1024]{0:T(1024)(128)(2,1)}, u32[]{:S(2)}) copy-start(bf16[1024]{0:T(1024)(128)(2,1)} %param.28) | copy-start | bytes 6148
  154.2 55.5 %all-gather.25.cloned.1.call-start = ((), (), s32[]{:S(2)}) async-start(), calls=%async_computation.22 | async-start | bytes 2359296 | tf_op jit(solution)/shard_map/all_gather | solution.py:327
  156.0 83.7 %all-gather.13.cloned.1.call-start = ((), (), s32[]{:S(2)}) async-start(), calls=%async_computation.13 | async-start | bytes 1310720 | tf_op jit(solution)/shard_map/all_gather | solution.py:309
  185.0 83.7 %all-gather.15.cloned.1.call-start = ((), (), s32[]{:S(2)}) async-start(), calls=%async_computation.15 | async-start | bytes 1310720 | tf_op jit(solution)/shard_map/all_gather | solution.py:309
  185.6 118.1 %reduce-scatter.15.cloned.1.call-start = ((), (), s32[]{:S(2)}) async-start(), calls=%async_computation.16 | async-start | bytes 1310720 | tf_op jit(solution)/shard_map/reduce_scatter | solution.py:315
  268.7 5.9 copy-start.8
  273.6 1.0 copy-start.24
  276.9 55.5 %reduce-scatter.13.cloned.1.call-start = ((), (), s32[]{:S(2)}) async-start(), calls=%async_computation.14 | async-start | bytes 1310720 | tf_op jit(solution)/shard_map/reduce_scatter | solution.py:315
  281.0 80.7 %copy-start.15 = (bf16[256,1024]{1,0:T(8,128)(2,1)S(1)}, bf16[256,1024]{1,0:T(8,128)(2,1)}, u32[]{:S(2)}) copy-start(bf16[256,1024]{1,0:T(8,128)(2,1)} %param.23) | copy-start | bytes 1572868
  281.0 80.7 %all-gather.17.cloned.1.call-start = ((), (), s32[]{:S(2)}) async-start(), calls=%async_computation.17 | async-start | bytes 1310720 | tf_op jit(solution)/shard_map/all_gather | solution.py:309
  363.4 11.0 %copy-start.3 = (f32[64,2048]{1,0:T(8,128)S(1)}, f32[64,2048]{1,0:T(8,128)}, u32[]{:S(2)}) copy-start(f32[64,2048]{1,0:T(8,128)} %copy-done.2) | copy-start | bytes 1572868
  411.2 4.0 copy-start.20
  411.2 21.9 %all-to-all-start.4 = ((bf16[8,2,320,128]{3,2,1,0:T(8,128)(2,1)}), bf16[8,2,320,128]{3,2,1,0:T(8,128)(2,1)S(1)}, u32[]{:S(2)}, u32[]{:S(2)}) async-start(bf16[8,2,320,128]{3,2,1,0:T(8,128)(2,1)} %bitcast.38), calls=%async_computation.7 | async-start | bytes 2621440 | tf_op jit(solution)/shard_map/all_to_all | solution.py:312
  415.0 131.1 %all-reduce.6.cloned.1.call-start = ((), (), s32[]{:S(2)}) async-start(), calls=%async_computation.23 | async-start | bytes 12582912
  415.2 4.0 copy-start.13
  415.2 4.0 copy-start.23
  419.3 3.0 copy-start.6
  419.3 3.0 copy-start.7
  443.3 1.1 copy-start.14
  443.4 4.6 copy-start.22
  443.4 155.9 %reduce-scatter.17.cloned.1.call-start = ((), (), s32[]{:S(2)}) async-start(), calls=%async_computation.18 | async-start | bytes 1310720 | tf_op jit(solution)/shard_map/reduce_scatter | solution.py:315
  447.9 134.8 %copy-start.4 = (bf16[1,2,1,64,1024]{4,3,2,1,0:T(8,128)(2,1)S(1)}, bf16[1,2,1,64,1024]{4,3,2,1,0:T(8,128)(2,1)}, u32[]{:S(2)}) copy-start(bf16[1,2,1,64,1024]{4,3,2,1,0:T(8,128)(2,1)} %param.16) | copy-start | bytes 786436
  447.9 198.8 %all-gather.19.cloned.1.call-start = ((), (), s32[]{:S(2)}) async-start(), calls=%async_computation.19 | async-start | bytes 1769472 | tf_op jit(solution)/shard_map/all_gather | solution.py:309
  563.8 86.5 %all-gather.21.cloned.1.call-start = ((), (), s32[]{:S(2)}) async-start(), calls=%async_computation.20 | async-start | bytes 2359296 | tf_op jit(solution)/shard_map/all_gather | solution.py:309
  582.9 56.7 %copy-start.9 = (f32[128,1024]{1,0:T(8,128)S(1)}, f32[128,1024]{1,0:T(8,128)}, u32[]{:S(2)}) copy-start(f32[128,1024]{1,0:T(8,128)} %get-tuple-element.131) | copy-start | bytes 1572868
  584.9 56.7 %copy-start.16 = (bf16[256,1024]{1,0:T(8,128)(2,1)S(1)}, bf16[256,1024]{1,0:T(8,128)(2,1)}, u32[]{:S(2)}) copy-start(bf16[256,1024]{1,0:T(8,128)(2,1)} %get-tuple-element.127) | copy-start | bytes 1572868
  646.8 7.7 %copy-start.1 = (bf16[1024,1024]{1,0:T(8,128)(2,1)S(1)}, bf16[1024,1024]{1,0:T(8,128)(2,1)}, u32[]{:S(2)}) copy-start(bf16[1024,1024]{1,0:T(8,128)(2,1)} %param.29) | copy-start | bytes 6291460
Sparse Core Ops, SparseCore 0:
  13.2 40.9 all-gather.10
  56.7 24.7 all-gather.22
  154.4 26.2 reduce-scatter.10
  183.1 26.5 all-gather.24
  211.8 27.9 all-gather.12
  241.2 27.4 all-gather.14
  277.0 26.6 reduce-scatter.14
  306.6 25.7 reduce-scatter.12
  335.1 26.5 all-gather.16
  443.5 102.4 all-reduce.5
  548.9 30.7 reduce-scatter.16
  582.2 26.8 all-gather.18
  611.8 28.5 all-gather.20

commit v2 on v1

--- a/solution.py
+++ b/solution.py
@@ -304,6 +304,7 @@
     ctx_index = lax.axis_index("ctx")
     group_index = lax.axis_index("fsdp")
     shard = width // groups
+    cut = w_qkv.shape[0] // ctx_size
 
     def gather(rows, axis_name):
         return lax.all_gather(rows, axis_name, axis=0, tiled=True)
@@ -316,19 +317,41 @@
             rows.astype(b16), "fsdp", scatter_dimension=0, tiled=True
         ).astype(f32)
 
-    cut = w_qkv.shape[0] // ctx_size
+    def dot_tn(left, right):
+        return lax.dot_general(
+            left, right, (((0,), (0,)), ((), ())), preferred_element_type=f32
+        ).astype(b16)
+
+    def spread(sums):
+        sums = sums.reshape(-1, shard).T
+        mine = jnp.arange(groups)[:, None, None] == group_index
+        return jnp.where(mine, sums[None], 0.0).reshape(width, -1)
+
+    def own_row_sums(cols, extras):
+        extra = jnp.concatenate(extras, axis=1)
+        extra = jnp.pad(extra, ((0, 0), (0, 128 - extra.shape[1]))).astype(b16)
+        total = cols.shape[1]
+        cols = jnp.concatenate([cols, extra], axis=1)
+        cols = cols.reshape(groups, ctx_size, cut, total + 128).transpose(1, 0, 2, 3)
+        terms = exchange(cols, "ctx")
+        moved = exchange(jnp.sum(terms.astype(f32), axis=0).astype(b16), "fsdp")
+        main = moved[:, :, :total].transpose(1, 0, 2).reshape(cut, groups * total)
+        rest = jnp.sum(moved[:, :, total:].astype(f32), axis=0).astype(b16)
+        whole = gather(jnp.concatenate([main, rest], axis=1), "ctx").astype(f32)
+        return whole[:, : groups * total], whole[:, groups * total :]
+
     cut_qkv = lax.dynamic_slice_in_dim(w_qkv, ctx_index * cut, cut).reshape(cut, groups, qkv_cols)
     cut_up = lax.dynamic_slice_in_dim(w_up, ctx_index * cut, cut).reshape(cut, groups, up_cols)
-    cut_both = exchange(
-        jnp.concatenate([cut_qkv, cut_up], axis=2).transpose(1, 0, 2), "fsdp"
-    )
+    cut_qkv = exchange(cut_qkv.transpose(1, 0, 2), "fsdp")
+    cut_qkv, cut_up = lax.optimization_barrier((cut_qkv, cut_up))
+    cut_up = exchange(cut_up.transpose(1, 0, 2), "fsdp")
 
     def own_columns(cut_cols):
         whole = lax.all_gather(cut_cols, "ctx", axis=0)
         return whole.transpose(1, 0, 2, 3).reshape(width, cut_cols.shape[2])
 
-    own_qkv = own_columns(cut_both[:, :, :qkv_cols])
-    own_up = own_columns(cut_both[:, :, qkv_cols:])
+    own_qkv = own_columns(cut_qkv)
+    own_up = own_columns(cut_up)
 
     own_rows = hidden.reshape(tok_rows, width)
     grad_out = d_output.reshape(tok_rows, width)
@@ -346,7 +369,8 @@
 
     rows_in = own_rows.astype(f32)
     normed_one, inv_one = norm_parts(rows_in)
-    first_in = (norm_parts(all_rows.astype(f32))[0] * full_g1 + full_b1).astype(b16)
+    normed_all = norm_parts(all_rows.astype(f32))[0]
+    first_in = (normed_all * full_g1 + full_b1).astype(b16)
     joined_bias = jnp.concatenate(
         [
             qv_bias[:, :head_width],
@@ -391,6 +415,7 @@
     part = (ctx_index % parts).astype(jnp.int32).reshape(1)
     slope = lax.dynamic_slice_in_dim(alibi_slopes, group_index * heads + ctx_index // parts, 1)
     out_packed, out_t, lse = attend(slots, part, slope, packed, block_span)
+    out_packed, own_up, all_grad = lax.optimization_barrier((out_packed, own_up, all_grad))
 
     attended = unpack_queries(
         exchange(out_packed.reshape(ctx_size, 2, half, 2 * head_width), "ctx")
@@ -401,14 +426,17 @@
     hidden_pre = dot_nn(second_in, own_up) + up_bias.astype(f32)
     activated, gelu_pull = jax.vjp(gelu_tanh, hidden_pre)
     activated = activated.astype(b16)
-    result = middle + scatter(dot_nn(activated, w_down)) + full_bd
-    output = result.astype(b16).reshape(hidden.shape)
-
     grad_act = dot_nt(all_grad, w_down).astype(b16)
     grad_pre = gelu_pull(grad_act.astype(f32))[0].astype(b16)
     grad_second = scatter(dot_nt(grad_pre, own_up))
     grad_middle = grad_out.astype(f32) + norm_back(grad_second, full_g2, normed_two, inv_two)
-    grad_branch = gather(grad_middle.astype(b16), "fsdp")
+    own_branch = grad_middle.astype(b16)
+    grad_branch = gather(own_branch, "fsdp")
+    down_term, grad_branch = lax.optimization_barrier(
+        (dot_nn(activated, w_down).astype(b16), grad_branch)
+    )
+    result = middle + scatter(down_term) + full_bd
+    output = result.astype(b16).reshape(hidden.shape)
     grad_attended = dot_nt(grad_branch, w_out).astype(b16)
     grad_packed = exchange(
         pack_queries(
@@ -420,6 +448,20 @@
     grads = exchange(
         grads.reshape(ctx_size, 2, block_span + half, 2 * head_width), "ctx"
     )
+    d_w_down, d_w_out = lax.psum(
+        (dot_tn(activated, all_grad), dot_tn(attended, grad_branch)), "ctx"
+    )
+    d_w_up, up_sums = own_row_sums(
+        dot_tn(second_in, grad_pre),
+        [
+            jnp.sum(grad_second * normed_two, axis=0)[:, None],
+            jnp.sum(grad_second, axis=0)[:, None],
+            jnp.sum(own_branch.astype(f32), axis=0)[:, None],
+            jnp.sum(grad_out.astype(f32), axis=0)[:, None],
+            spread(jnp.sum(grad_pre.astype(f32), axis=0)),
+        ],
+    )
+    grads, d_w_down, d_w_out = lax.optimization_barrier((grads, d_w_down, d_w_out))
     grad_q = unpack_queries(grads[:, :, block_span:]).reshape(span, heads, head_width)
     grad_kv = jnp.sum(
         grads[:, :, :block_span]
@@ -429,82 +471,40 @@
     ).astype(b16)
     grad_kv = grad_kv.transpose(2, 1, 3, 0, 4).reshape(span, heads, 2 * head_width)
     grad_joined = jnp.concatenate([grad_q, grad_kv], axis=2).reshape(span, qkv_cols)
-    grad_first = scatter(dot_nt(grad_joined, own_qkv))
+    first_term = dot_nt(grad_joined, own_qkv)
+    grad_first = scatter(first_term)
     grad_rows = grad_middle + norm_back(grad_first, full_g1, normed_one, inv_one)
     d_hidden = grad_rows.astype(b16).reshape(hidden.shape)
 
-    def dot_tn(left, right):
-        return lax.dot_general(
-            left, right, (((0,), (0,)), ((), ())), preferred_element_type=f32
-        ).astype(b16)
-
-    def own_row_sums(cols):
-        cols = cols.reshape(groups, ctx_size, cut, cols.shape[1]).transpose(1, 0, 2, 3)
-        summed = lax.psum_scatter(cols, "ctx", scatter_dimension=0, tiled=True)
-        moved = exchange(summed[0], "fsdp").transpose(1, 0, 2)
-        return gather(moved.reshape(cut, -1), "ctx").astype(f32)
-
-    d_w_down, d_w_out = lax.psum(
-        (dot_tn(activated, all_grad), dot_tn(attended, grad_branch)), "ctx"
-    )
-    d_w_up = own_row_sums(dot_tn(second_in, grad_pre))
-    d_w_qkv = own_row_sums(dot_tn(first_in, grad_joined))
-
-    def own_sum(rows):
-        return lax.dynamic_slice_in_dim(
-            jnp.sum(rows.astype(f32), axis=0), group_index * shard, shard
-        )
-
     joined_sums = jnp.sum(grad_joined.astype(f32), axis=0).reshape(heads, 3, head_width)
     sum_qv = jnp.concatenate([joined_sums[:, 0], joined_sums[:, 2]], axis=1)
-    early = lax.psum(
-        jnp.concatenate(
-            [
-                jnp.sum(grad_pre.astype(f32), axis=0),
-                own_sum(grad_branch),
-                own_sum(all_grad),
-            ]
-        ),
-        "ctx",
-    )
-    d_up_bias = early[:up_cols]
-    d_out_bias = early[up_cols : up_cols + shard]
-    d_down_bias = early[up_cols + shard :]
-    spread = jnp.where(
-        jnp.arange(groups)[:, None] == group_index, sum_qv.reshape(1, -1), 0.0
-    ).reshape(-1)
-    late = lax.psum(
-        jnp.concatenate(
-            [
-                jnp.sum(grad_first * normed_one, axis=0),
-                jnp.sum(grad_first, axis=0),
-                jnp.sum(grad_second * normed_two, axis=0),
-                jnp.sum(grad_second, axis=0),
-                spread,
-            ]
-        ),
-        ("ctx", "fsdp"),
-    )
-    norm_sums = late[: 4 * width].reshape(4, groups, shard)
-    norm_sums = lax.dynamic_slice_in_dim(norm_sums, group_index, 1, axis=1)[:, 0]
-    d_qv_bias = lax.dynamic_slice_in_dim(
-        late[4 * width :].reshape((groups,) + sum_qv.shape), group_index, 1
-    )[0]
+    d_w_qkv, qkv_sums = own_row_sums(
+        dot_tn(first_in, grad_joined),
+        [
+            jnp.sum(first_term * normed_all, axis=0)[:, None],
+            jnp.sum(first_term, axis=0)[:, None],
+            spread(sum_qv.reshape(-1)),
+        ],
+    )
+    qv_lanes = sum_qv.size // shard
+    d_qv_bias = qkv_sums[:, 2 : 2 + qv_lanes].T.reshape(sum_qv.shape)
+    up_lanes = up_cols // shard
+    d_up_bias = up_sums[:, 4 : 4 + up_lanes].T.reshape(up_cols)
     return (
         output,
         d_hidden,
-        norm_sums[0],
-        norm_sums[1],
+        qkv_sums[:, 0],
+        qkv_sums[:, 1],
         d_w_qkv,
         d_qv_bias,
         d_w_out.astype(f32),
-        d_out_bias,
-        norm_sums[2],
-        norm_sums[3],
+        up_sums[:, 2],
+        up_sums[:, 0],
+        up_sums[:, 1],
         d_w_up,
         d_up_bias,
         d_w_down.astype(f32),
-        d_down_bias,
+        up_sums[:, 3],
     )
 
 

time: 662 us -> 532 us (0.80)
  waiting for transfers between devices: 331 us -> 221 us
  blocking collectives: 132 us -> 84.6 us
  local copies, waits for them, and re-layouts: 37.6 us -> 53 us
  starting transfers between devices: 8.21 us -> 22.5 us
    unnamed x14 -> x13, waiting for transfers between devices: 98.2 us -> 1.38 us
    psum x2 -> x0, blocking collectives: 50.2 us -> none  [the longest x1 37.9 us: local(): lax.psum(jnp.concatenate([jnp.sum(grad_first * normed_one, axis=0), jnp.s...]
    all_to_all x2 -> x5, waiting for transfers between devices: 26.8 us -> 65.1 us  [exchange(): lax.all_to_all(rows, axis_name, split_axis=0, concat_axis=0, tiled=True)]
    all_gather x6, waiting for transfers between devices: 84.4 us -> 50.2 us  [gather(): return lax.all_gather(rows, axis_name, axis=0, tiled=True)]
    psum x0 -> x1, waiting for transfers between devices: none -> 28.2 us  [local(): lax.psum((dot_tn(activated, all_grad), dot_tn(attended, grad_branch)), 'c...]
    all_gather x2, waiting for transfers between devices: 47.4 us -> 22.8 us  [own_columns(): whole = lax.all_gather(cut_cols, 'ctx', axis=0)]
    reduce_scatter x4, waiting for transfers between devices: 74.4 us -> 53.1 us  [scatter(): lax.psum_scatter(rows.astype(b16), 'fsdp', scatter_dimension=0, tiled=True)]
    all_to_all x2 -> x5, starting transfers between devices: 7.27 us -> 21.6 us  [exchange(): lax.all_to_all(rows, axis_name, split_axis=0, concat_axis=0, tiled=True)]
  transfers between devices with their start and end apart: 15 -> 18, of which waited for: 12 -> 12; matrix products, arithmetic and copies ran while one was open for 9% -> 14% of each run, Pallas kernels for 0% -> 12%
where the time goes in v2:
time: 532 us; the launch traced here: 530 us
  waiting for transfers between devices  221 us (42%)
  blocking collectives  84.6 us (16%)
  Pallas kernels  62.7 us (12%)
  local copies, waits for them, and re-layouts  53 us (10%)
  other arithmetic  38.7 us (7%)
  matrix products  33.4 us (6%)
  starting transfers between devices  22.5 us (4%)
  between operations  14.6 us (3%)
    all_to_all x5, blocking collectives, exchange(): lax.all_to_all(rows, axis_name, split_axis=0, concat_axis=0, tiled=True)  84.6 us
    all_to_all x5, waiting for transfers between devices, exchange(): lax.all_to_all(rows, axis_name, split_axis=0, concat_axis=0, tiled=True)  65.1 us
    reduce_scatter x4, waiting for transfers between devices, scatter(): lax.psum_scatter(rows.astype(b16), 'fsdp', scatter_dimension=0, tiled=True)  53.1 us
    all_gather x6, waiting for transfers between devices, gather(): return lax.all_gather(rows, axis_name, axis=0, tiled=True)  50.2 us
    pallas_call x1, Pallas kernels, attend_back(): pl.pallas_call(functools.partial(attend_back_kernel, block_span), out_sha...  36.8 us
    psum x1, waiting for transfers between devices, local(): lax.psum((dot_tn(activated, all_grad), dot_tn(attended, grad_branch)), 'c...  28.2 us
    pallas_call x1, Pallas kernels, attend(): pl.pallas_call(functools.partial(attend_kernel, block_span), out_shape=(j...  25.9 us
    all_gather x2, waiting for transfers between devices, own_columns(): whole = lax.all_gather(cut_cols, 'ctx', axis=0)  22.8 us
  transfers between devices with their start and end apart: 18, of which 12 were waited for; matrix products, arithmetic and copies ran while one was open for 14% of the time, Pallas kernels for 12%

profile of v2, /device:TPU:0, one launch (start us, length us, event | category | flops | bytes accessed | tf_op | source)
XLA Modules:
  0.0 530.3 jit_solution(13701440681482653834)
XLA Ops:
  11.4 1.7 fusion.38
  14.9 6.3 %all-to-all-start = ((bf16[4,32,768]{2,1,0:T(8,128)(2,1)}), bf16[4,32,768]{2,1,0:T(8,128)(2,1)S(1)}, u32[]{:S(2)}, u32[]{:S(2)}) async-start(bf16[4,32,768]{2,1,0:T(8,128)(2,1)} %copy.161), calls=%async_computation | async-start | bytes 393216 | tf_op jit(solution)/shard_map/all_to_all | solution.py:313
  22.3 9.3 %all-to-all-done = bf16[4,32,768]{2,1,0:T(8,128)(2,1)S(1)} async-done(((bf16[4,32,768]{2,1,0:T(8,128)(2,1)}), bf16[4,32,768]{2,1,0:T(8,128)(2,1)S(1)}, u32[]{:S(2)}, u32[]{:S(2)}) %all-to-all-start) | async-done | bytes 196640 | tf_op jit(solution)/shard_map/all_to_all | solution.py:313
  32.5 19.5 %all_to_all.50 = bf16[4,32,1024]{2,1,0:T(8,128)(2,1)} all-to-all(bf16[4,32,1024]{2,1,0:T(8,128)(2,1)S(1)} %copy.165), channel_id=1, replica_groups=mesh['ctx'=8,'fsdp'=4] {'fsdp'}, dimensions={0} | all-to-all | bytes 524288 | tf_op jit(solution)/shard_map/all_to_all | solution.py:313
  53.7 1.5 convert_reduce_fusion.2
  55.9 1.6 multiply_reduce_fusion
  58.1 22.8 %all-gather.23.cloned.1.call-done = bf16[32,32,768]{2,1,0:T(8,128)(2,1)} async-done(((bf16[4,32,768]{2,1,0:T(8,128)(2,1)}), bf16[32,32,768]{2,1,0:T(8,128)(2,1)}) %all-gather.23.cloned.1.call-update) | async-done | bytes 1572880 | tf_op jit(solution)/shard_map/all_gather | solution.py:350
  80.9 1.5 copy.162
  83.6 1.9 add_convert_fusion.1
  85.5 2.7 reshape.324
  89.2 1.3 maximum_maximum_fusion
  90.5 3.6 all-to-all-start.1
  95.1 22.8 %all-to-all-done.1 = bf16[8,2,320,128]{3,2,1,0:T(8,128)(2,1)S(1)} async-done(((bf16[8,2,320,128]{3,2,1,0:T(8,128)(2,1)}), bf16[8,2,320,128]{3,2,1,0:T(8,128)(2,1)S(1)}, u32[]{:S(2)}, u32[]{:S(2)}) %all-to-all-start.1) | async-done | bytes 1310752 | tf_op jit(solution)/shard_map/all_to_all | solution.py:313
  117.9 25.9 %attend.1 = (bf16[16,64,128]{2,1,0:T(8,128)(2,1)S(1)}, f32[64,2048]{1,0:T(8,128)S(1)}, f32[1,2048]{1,0:T(1,128)S(1)}) custom-call(s32[16]{0:T(128)S(1)} %select_reduce_fusion.slots, s32[1]{0:T(128)} %bitcast.1.part, f32[1]{0:T(128)} %dynamic_slice.9.slope, bf16[16,320,128]{2,1,0:T(8,128)(2,1)S(1)} %bitcast.145), custom_call_target="tpu_custom_call" | custom-call | flops 2147483648 | bytes 2621440 | tf_op jit(solution)/shard_map/attend/pallas_call | solution.py:216
  145.3 3.2 copy.166
  148.5 10.3 %all_to_all.51 = bf16[8,2,64,128]{3,2,1,0:T(8,128)(2,1)S(1)} all-to-all(bf16[8,2,64,128]{3,2,1,0:T(8,128)(2,1)} %bitcast.148), channel_id=1, replica_groups=mesh['ctx'=8,'fsdp'=4] {'ctx'}, dimensions={0} | all-to-all | bytes 524288 | tf_op jit(solution)/shard_map/all_to_all | solution.py:313
  159.0 1.2 copy.167
  160.2 2.2 reshape.331
  162.3 2.5 convolution_convert_fusion.6
  165.0 26.4 %reduce-scatter.5.cloned.1.call-done = bf16[128,1024]{1,0:T(8,128)(2,1)} async-done(((bf16[512,1024]{1,0:T(8,128)(2,1)}), bf16[128,1024]{1,0:T(8,128)(2,1)}) %reduce-scatter.5.cloned.1.call-update) | async-done | bytes 262160 | tf_op jit(solution)/shard_map/reduce_scatter | solution.py:316
  191.3 1.2 fusion.41
  192.5 1.2 multiply_reduce_fusion.1
  193.8 1.9 add_convert_fusion.3
  195.9 26.5 %all-gather.15.cloned.1.call-done = bf16[512,1024]{1,0:T(8,128)(2,1)} async-done(((bf16[128,1024]{1,0:T(8,128)(2,1)}), bf16[512,1024]{1,0:T(8,128)(2,1)}) %all-gather.15.cloned.1.call-update) | async-done | bytes 1048592 | tf_op jit(solution)/shard_map/all_gather | solution.py:310
  222.4 3.2 fusion.51
  225.7 2.9 convert_reduce_fusion
  229.6 2.3 convolution_convert_fusion.3
  231.9 26.7 %reduce-scatter.7.cloned.1.call-done = bf16[128,1024]{1,0:T(8,128)(2,1)} async-done(((bf16[512,1024]{1,0:T(8,128)(2,1)}), bf16[128,1024]{1,0:T(8,128)(2,1)}) %reduce-scatter.7.cloned.1.call-update) | async-done | bytes 262160 | tf_op jit(solution)/shard_map/reduce_scatter | solution.py:316
  258.7 1.4 fusion.31
  260.1 2.4 fusion.44
  262.6 5.0 convolution_convert_fusion.1
  267.6 2.5 convolution_convert_fusion.5
  270.1 19.3 %all-gather.17.cloned.1.call-done = bf16[512,1024]{1,0:T(8,128)(2,1)} async-done(((bf16[128,1024]{1,0:T(8,128)(2,1)}), bf16[512,1024]{1,0:T(8,128)(2,1)}) %all-gather.17.cloned.1.call-update) | async-done | bytes 1048592 | tf_op jit(solution)/shard_map/all_gather | solution.py:310
  289.3 1.8 convolution_convert_fusion.8
  292.5 3.6 all-to-all-start.4
  296.2 2.5 convolution_convert_fusion.7
  298.8 4.3 all-to-all-done.4
  303.1 36.8 %attend_back.1 = bf16[16,320,128]{2,1,0:T(8,128)(2,1)} custom-call(s32[16]{0:T(128)S(1)} %select_reduce_fusion.slots, s32[1]{0:T(128)} %bitcast.1.part, f32[1]{0:T(128)} %dynamic_slice.9.slope, bf16[16,320,128]{2,1,0:T(8,128)(2,1)S(1)} %bitcast.146, bf16[16,64,128]{2,1,0:T(8,128)(2,1)S(1)} %bitcast.147, f32[64,2048]{1,0:T(8,128)S(1)} %copy-done.4, ...), custom_call_target="tpu_custom_call" | custom-call | flops 2684354560 | bytes 5242880 | tf_op jit(solution)/shard_map/attend_back/pallas_call | solution.py:246
  339.9 3.7 all-to-all-start.5
  344.1 28.2 %all-reduce.6.cloned.1.call-done = (bf16[1024,1024]{1,0:T(8,128)(2,1)}, bf16[256,1024]{1,0:T(8,128)(2,1)}) async-done(((bf16[1024,1024]{1,0:T(8,128)(2,1)}, bf16[256,1024]{1,0:T(8,128)(2,1)}), (bf16[1024,1024]{1,0:T(8,128)(2,1)}, bf16[256,1024]{1,0:T(8,128)(2,1)})) %all-reduce.6.cloned.1.call-update) | async-done | bytes 2621456 | tf_op jit(solution)/shard_map/psum | solution.py:451
  373.0 1.4 pad_maximum_fusion.1
  374.4 1.5 copy.172
  375.8 3.6 fusion.13
  379.5 4.2 convolution_convert_fusion
  383.7 3.2 fusion.1
  387.0 4.3 copy.179
  391.2 3.3 copy.180
  394.6 4.4 all-to-all-start.8
  399.7 28.7 %all-to-all-done.8 = bf16[8,4,32,1152]{3,2,1,0:T(8,128)(2,1)} async-done(((bf16[8,4,32,1152]{3,2,1,0:T(8,128)(2,1)}), bf16[8,4,32,1152]{3,2,1,0:T(8,128)(2,1)}, u32[]{:S(2)}, u32[]{:S(2)}) %all-to-all-start.8) | async-done | bytes 2359328 | tf_op jit(solution)/shard_map/all_to_all | solution.py:313
  428.4 2.1 reduce_sum.253
  430.5 10.9 %all_to_all.52 = bf16[4,32,1152]{2,1,0:T(8,128)(2,1)S(1)} all-to-all(bf16[4,32,1152]{2,1,0:T(8,128)(2,1)S(1)} %reduce_sum.253), channel_id=1, replica_groups=mesh['ctx'=8,'fsdp'=4] {'fsdp'}, dimensions={0} | all-to-all | bytes 589824 | tf_op jit(solution)/shard_map/all_to_all | solution.py:313
  444.2 2.5 copy.174
  446.6 1.7 copy.175
  448.4 33.3 %all_to_all.53 = bf16[8,4,32,896]{3,2,1,0:T(8,128)(2,1)S(1)} all-to-all(bf16[8,4,32,896]{3,2,1,0:T(8,128)(2,1)S(1)} %copy.175), channel_id=1, replica_groups=mesh['ctx'=8,'fsdp'=4] {'ctx'}, dimensions={0} | all-to-all | bytes 3670016 | tf_op jit(solution)/shard_map/all_to_all | solution.py:313
  481.9 10.7 %all_to_all.54 = bf16[4,32,896]{2,1,0:T(8,128)(2,1)S(1)} all-to-all(bf16[4,32,896]{2,1,0:T(8,128)(2,1)S(1)} %reduce_sum.246), channel_id=1, replica_groups=mesh['ctx'=8,'fsdp'=4] {'fsdp'}, dimensions={0} | all-to-all | bytes 458752 | tf_op jit(solution)/shard_map/all_to_all | solution.py:313
  495.0 4.1 convert_element_type.201
  500.4 2.1 fusion.26
  502.5 1.9 convert_element_type.200
  504.4 2.0 copy-done.9
  507.2 4.1 slice.196
  511.3 2.2 slice_reduce_fusion
  513.5 3.6 all-gather.19.cloned.1.call-done
  517.1 1.6 convert_element_type.194
  520.3 3.5 slice.189
  (187 shorter events, 29.3 us)
Async XLA Ops:
  7.2 218.5 %copy-start = (bf16[1024,1024]{1,0:T(8,128)(2,1)S(1)}, bf16[1024,1024]{1,0:T(8,128)(2,1)}, u32[]{:S(2)}) copy-start(bf16[1024,1024]{1,0:T(8,128)(2,1)} %param.29) | copy-start | bytes 6291460
  7.2 46.5 %all-gather.11.cloned.1.call-start = ((), (), s32[]{:S(2)}) async-start(), calls=%async_computation.14 | async-start | bytes 1474560 | tf_op jit(solution)/shard_map/all_gather | solution.py:310
  14.0 38.6 %copy-start.19 = (bf16[4,128]{1,0:T(4,128)(2,1)S(1)}, bf16[4,128]{1,0:T(4,128)(2,1)}, u32[]{:S(2)}) copy-start(bf16[4,128]{1,0:T(4,128)(2,1)} %param.22) | copy-start | bytes 3076
  14.9 16.8 %all-to-all-start = ((bf16[4,32,768]{2,1,0:T(8,128)(2,1)}), bf16[4,32,768]{2,1,0:T(8,128)(2,1)S(1)}, u32[]{:S(2)}, u32[]{:S(2)}) async-start(bf16[4,32,768]{2,1,0:T(8,128)(2,1)} %copy.161), calls=%async_computation | async-start | bytes 393216 | tf_op jit(solution)/shard_map/all_to_all | solution.py:313
  21.2 59.7 %all-gather.23.cloned.1.call-start = ((), (), s32[]{:S(2)}) async-start(), calls=%async_computation.24 | async-start | bytes 1769472 | tf_op jit(solution)/shard_map/all_gather | solution.py:350
  31.6 0.7 copy-start.17
  32.3 112.9 %all-gather.25.cloned.1.call-start = ((), (), s32[]{:S(2)}) async-start(), calls=%async_computation.25 | async-start | bytes 2359296 | tf_op jit(solution)/shard_map/all_gather | solution.py:350
  52.0 96.4 %all-gather.13.cloned.1.call-start = ((), (), s32[]{:S(2)}) async-start(), calls=%async_computation.15 | async-start | bytes 1310720 | tf_op jit(solution)/shard_map/all_gather | solution.py:310
  53.7 3.9 copy-start.7
  58.1 24.4 %copy-start.15 = (bf16[4,128,1024]{2,1,0:T(8,128)(2,1)}, bf16[4,128,1024]{2,1,0:T(8,128)(2,1)S(1)}, u32[]{:S(2)}) copy-start(bf16[4,128,1024]{2,1,0:T(8,128)(2,1)S(1)} %add_convert_fusion) | copy-start | bytes 3145732
  82.4 1.1 copy-start.14
  89.2 5.0 copy-start.21
  89.2 5.1 copy-start.23
  90.5 27.3 %all-to-all-start.1 = ((bf16[8,2,320,128]{3,2,1,0:T(8,128)(2,1)}), bf16[8,2,320,128]{3,2,1,0:T(8,128)(2,1)S(1)}, u32[]{:S(2)}, u32[]{:S(2)}) async-start(bf16[8,2,320,128]{3,2,1,0:T(8,128)(2,1)} %maximum_maximum_fusion), calls=%async_computation.1 | async-start | bytes 2621440 | tf_op jit(solution)/shard_map/all_to_all | solution.py:313
  94.1 97.2 %reduce-scatter.5.cloned.1.call-start = ((), (), s32[]{:S(2)}) async-start(), calls=%async_computation.16 | async-start | bytes 1310720 | tf_op jit(solution)/shard_map/reduce_scatter | solution.py:316
  143.8 0.7 copy-start.2
  144.5 0.8 copy-start.3
  162.3 33.6 %copy-start.20 = (bf16[1024]{0:T(1024)(128)(2,1)S(1)}, bf16[1024]{0:T(1024)(128)(2,1)}, u32[]{:S(2)}) copy-start(bf16[1024]{0:T(1024)(128)(2,1)} %param.28) | copy-start | bytes 6148
  164.9 57.5 %all-gather.15.cloned.1.call-start = ((), (), s32[]{:S(2)}) async-start(), calls=%async_computation.17 | async-start | bytes 1310720 | tf_op jit(solution)/shard_map/all_gather | solution.py:310
  195.7 63.0 %reduce-scatter.7.cloned.1.call-start = ((), (), s32[]{:S(2)}) async-start(), calls=%async_computation.18 | async-start | bytes 1310720 | tf_op jit(solution)/shard_map/reduce_scatter | solution.py:316
  222.4 3.3 copy-start.22
  225.7 2.9 copy-start.24
  225.7 3.9 copy-start.13
  228.6 1.0 copy-start.26
  231.9 57.5 %all-gather.17.cloned.1.call-start = ((), (), s32[]{:S(2)}) async-start(), calls=%async_computation.19 | async-start | bytes 1310720 | tf_op jit(solution)/shard_map/all_gather | solution.py:310
  262.6 5.0 copy-start.25
  291.2 5.0 copy-start.10
  292.5 10.6 %all-to-all-start.4 = ((bf16[8,2,64,128]{3,2,1,0:T(8,128)(2,1)}), bf16[8,2,64,128]{3,2,1,0:T(8,128)(2,1)S(1)}, u32[]{:S(2)}, u32[]{:S(2)}) async-start(bf16[8,2,64,128]{3,2,1,0:T(8,128)(2,1)} %pad_maximum_fusion.3), calls=%async_computation.7 | async-start | bytes 524288 | tf_op jit(solution)/shard_map/all_to_all | solution.py:313
  296.1 6.9 %copy-start.4 = (f32[64,2048]{1,0:T(8,128)S(1)}, f32[64,2048]{1,0:T(8,128)}, u32[]{:S(2)}) copy-start(f32[64,2048]{1,0:T(8,128)} %copy-done.3) | copy-start | bytes 1572868
  296.1 76.1 %all-reduce.6.cloned.1.call-start = ((), (), s32[]{:S(2)}) async-start(), calls=%async_computation.26 | async-start | bytes 5242880 | tf_op jit(solution)/shard_map/psum | solution.py:451
  339.9 4.0 copy-start.11
  339.9 32.4 %all-to-all-start.5 = ((bf16[8,2,320,128]{3,2,1,0:T(8,128)(2,1)}), bf16[8,2,320,128]{3,2,1,0:T(8,128)(2,1)S(1)}, u32[]{:S(2)}, u32[]{:S(2)}) async-start(bf16[8,2,320,128]{3,2,1,0:T(8,128)(2,1)} %bitcast.39), calls=%async_computation.8 | async-start | bytes 2621440 | tf_op jit(solution)/shard_map/all_to_all | solution.py:313
  343.6 155.6 %reduce-scatter.11.cloned.1.call-start = ((), (), s32[]{:S(2)}) async-start(), calls=%async_computation.21 | async-start | bytes 1310720 | tf_op jit(solution)/shard_map/reduce_scatter | solution.py:316
  373.0 2.9 copy-start.8
  394.6 33.8 %all-to-all-start.8 = ((bf16[8,4,32,1152]{3,2,1,0:T(8,128)(2,1)}), bf16[8,4,32,1152]{3,2,1,0:T(8,128)(2,1)}, u32[]{:S(2)}, u32[]{:S(2)}) async-start(bf16[8,4,32,1152]{3,2,1,0:T(8,128)(2,1)} %copy.180), calls=%async_computation.12 | async-start | bytes 4718592 | tf_op jit(solution)/shard_map/all_to_all | solution.py:313
  398.9 101.4 %reduce-scatter.9.cloned.1.call-start = ((), (), s32[]{:S(2)}) async-start(), calls=%async_computation.20 | async-start | bytes 1310720 | tf_op jit(solution)/shard_map/reduce_scatter | solution.py:316
  399.7 102.8 %all-gather.21.cloned.1.call-start = ((), (), s32[]{:S(2)}) async-start(), calls=%async_computation.23 | async-start | bytes 2433024 | tf_op jit(solution)/shard_map/all_gather | solution.py:310
  441.4 1.7 copy-start.16
  442.2 74.9 %all-gather.19.cloned.1.call-start = ((), (), s32[]{:S(2)}) async-start(), calls=%async_computation.22 | async-start | bytes 1843200 | tf_op jit(solution)/shard_map/all_gather | solution.py:310
  481.6 11.8 %copy-start.5 = (bf16[1,2,1,64,1024]{4,3,2,1,0:T(8,128)(2,1)S(1)}, bf16[1,2,1,64,1024]{4,3,2,1,0:T(8,128)(2,1)}, u32[]{:S(2)}) copy-start(bf16[1,2,1,64,1024]{4,3,2,1,0:T(8,128)(2,1)} %param.16) | copy-start | bytes 786436
  481.6 12.3 %copy-start.18 = (bf16[256,1024]{1,0:T(8,128)(2,1)S(1)}, bf16[256,1024]{1,0:T(8,128)(2,1)}, u32[]{:S(2)}) copy-start(bf16[256,1024]{1,0:T(8,128)(2,1)} %get-tuple-element.38) | copy-start | bytes 1572868
  495.0 5.4 %copy-start.6 = (bf16[128,1024]{1,0:T(8,128)(2,1)S(1)}, bf16[128,1024]{1,0:T(8,128)(2,1)}, u32[]{:S(2)}) copy-start(bf16[128,1024]{1,0:T(8,128)(2,1)} %reduce-scatter.5.cloned.1.call-done) | copy-start | bytes 786436
  495.0 5.4 %copy-start.12 = (f32[128,1024]{1,0:T(8,128)S(1)}, f32[128,1024]{1,0:T(8,128)}, u32[]{:S(2)}) copy-start(f32[128,1024]{1,0:T(8,128)} %get-tuple-element.169) | copy-start | bytes 1572868
  504.4 2.0 copy-start.9
  519.7 4.1 copy-start.1
Sparse Core Ops, SparseCore 0:
  13.2 40.4 all-gather.10
  56.1 24.7 all-gather.22
  82.8 33.5 all-gather.24
  117.8 30.0 all-gather.12
  165.0 26.2 reduce-scatter.4
  195.8 26.5 all-gather.14
  232.0 26.6 reduce-scatter.6
  262.7 26.5 all-gather.16
  300.9 71.3 all-reduce.5
  379.6 25.4 reduce-scatter.10
  407.5 25.7 reduce-scatter.8
  442.3 38.8 all-gather.20
  493.5 23.5 all-gather.18

commit v3 on v2

--- a/solution.py
+++ b/solution.py
@@ -327,18 +327,23 @@
         mine = jnp.arange(groups)[:, None, None] == group_index
         return jnp.where(mine, sums[None], 0.0).reshape(width, -1)
 
-    def own_row_sums(cols, extras):
+    def ctx_terms(cols):
+        cols = cols.reshape(groups, ctx_size, cut, cols.shape[1]).transpose(1, 0, 2, 3)
+        return exchange(cols, "ctx")
+
+    def to_owners(terms):
+        return exchange(jnp.sum(terms.astype(f32), axis=0).astype(b16), "fsdp")
+
+    def own_row_sums(cols, extras, ahead):
         extra = jnp.concatenate(extras, axis=1)
         extra = jnp.pad(extra, ((0, 0), (0, 128 - extra.shape[1]))).astype(b16)
         total = cols.shape[1]
-        cols = jnp.concatenate([cols, extra], axis=1)
-        cols = cols.reshape(groups, ctx_size, cut, total + 128).transpose(1, 0, 2, 3)
-        terms = exchange(cols, "ctx")
-        moved = exchange(jnp.sum(terms.astype(f32), axis=0).astype(b16), "fsdp")
+        moved = to_owners(ctx_terms(jnp.concatenate([cols, extra], axis=1)))
+        moved, ahead = lax.optimization_barrier((moved, ahead))
         main = moved[:, :, :total].transpose(1, 0, 2).reshape(cut, groups * total)
         rest = jnp.sum(moved[:, :, total:].astype(f32), axis=0).astype(b16)
         whole = gather(jnp.concatenate([main, rest], axis=1), "ctx").astype(f32)
-        return whole[:, : groups * total], whole[:, groups * total :]
+        return whole[:, : groups * total], whole[:, groups * total :], ahead
 
     cut_qkv = lax.dynamic_slice_in_dim(w_qkv, ctx_index * cut, cut).reshape(cut, groups, qkv_cols)
     cut_up = lax.dynamic_slice_in_dim(w_up, ctx_index * cut, cut).reshape(cut, groups, up_cols)
@@ -428,15 +433,21 @@
     activated = activated.astype(b16)
     grad_act = dot_nt(all_grad, w_down).astype(b16)
     grad_pre = gelu_pull(grad_act.astype(f32))[0].astype(b16)
+    down_terms = exchange(dot_tn(activated, all_grad).reshape(ctx_size, -1, width), "ctx")
     grad_second = scatter(dot_nt(grad_pre, own_up))
+    grad_second, down_terms = lax.optimization_barrier((grad_second, down_terms))
+    up_terms = ctx_terms(dot_tn(second_in, grad_pre))
     grad_middle = grad_out.astype(f32) + norm_back(grad_second, full_g2, normed_two, inv_two)
     own_branch = grad_middle.astype(b16)
     grad_branch = gather(own_branch, "fsdp")
-    down_term, grad_branch = lax.optimization_barrier(
-        (dot_nn(activated, w_down).astype(b16), grad_branch)
-    )
-    result = middle + scatter(down_term) + full_bd
-    output = result.astype(b16).reshape(hidden.shape)
+    down_sum = jnp.sum(down_terms.astype(f32), axis=0).astype(b16)
+    down_term, grad_branch, up_terms, down_sum = lax.optimization_barrier(
+        (dot_nn(activated, w_down).astype(b16), grad_branch, up_terms, down_sum)
+    )
+    d_w_out = lax.psum(dot_tn(attended, grad_branch), "ctx")
+    d_w_down = gather(down_sum, "ctx")
+    moved_up = to_owners(up_terms)
+    down_added = scatter(down_term)
     grad_attended = dot_nt(grad_branch, w_out).astype(b16)
     grad_packed = exchange(
         pack_queries(
@@ -445,21 +456,10 @@
         "ctx",
     ).reshape(2 * ctx_size, half, 2 * head_width)
     grads = attend_back(slots, part, slope, packed, grad_packed, out_t, lse, block_span)
+    grads, moved_up = lax.optimization_barrier((grads, moved_up))
+    d_w_up = gather(moved_up.transpose(1, 0, 2).reshape(cut, groups * up_cols), "ctx")
     grads = exchange(
         grads.reshape(ctx_size, 2, block_span + half, 2 * head_width), "ctx"
-    )
-    d_w_down, d_w_out = lax.psum(
-        (dot_tn(activated, all_grad), dot_tn(attended, grad_branch)), "ctx"
-    )
-    d_w_up, up_sums = own_row_sums(
-        dot_tn(second_in, grad_pre),
-        [
-            jnp.sum(grad_second * normed_two, axis=0)[:, None],
-            jnp.sum(grad_second, axis=0)[:, None],
-            jnp.sum(own_branch.astype(f32), axis=0)[:, None],
-            jnp.sum(grad_out.astype(f32), axis=0)[:, None],
-            spread(jnp.sum(grad_pre.astype(f32), axis=0)),
-        ],
     )
     grads, d_w_down, d_w_out = lax.optimization_barrier((grads, d_w_down, d_w_out))
     grad_q = unpack_queries(grads[:, :, block_span:]).reshape(span, heads, head_width)
@@ -478,33 +478,41 @@
 
     joined_sums = jnp.sum(grad_joined.astype(f32), axis=0).reshape(heads, 3, head_width)
     sum_qv = jnp.concatenate([joined_sums[:, 0], joined_sums[:, 2]], axis=1)
-    d_w_qkv, qkv_sums = own_row_sums(
+    d_w_qkv, qkv_sums, (d_w_up, down_added) = own_row_sums(
         dot_tn(first_in, grad_joined),
         [
             jnp.sum(first_term * normed_all, axis=0)[:, None],
             jnp.sum(first_term, axis=0)[:, None],
+            jnp.sum(grad_second * normed_two, axis=0)[:, None],
+            jnp.sum(grad_second, axis=0)[:, None],
+            jnp.sum(own_branch.astype(f32), axis=0)[:, None],
+            jnp.sum(grad_out.astype(f32), axis=0)[:, None],
+            spread(jnp.sum(grad_pre.astype(f32), axis=0)),
             spread(sum_qv.reshape(-1)),
         ],
-    )
+        (d_w_up, down_added),
+    )
+    sums = qkv_sums[:, :32].T
+    output = (middle + down_added + full_bd).astype(b16).reshape(hidden.shape)
     qv_lanes = sum_qv.size // shard
-    d_qv_bias = qkv_sums[:, 2 : 2 + qv_lanes].T.reshape(sum_qv.shape)
     up_lanes = up_cols // shard
-    d_up_bias = up_sums[:, 4 : 4 + up_lanes].T.reshape(up_cols)
+    d_up_bias = sums[6 : 6 + up_lanes].reshape(up_cols)
+    d_qv_bias = sums[6 + up_lanes : 6 + up_lanes + qv_lanes].reshape(sum_qv.shape)
     return (
         output,
         d_hidden,
-        qkv_sums[:, 0],
-        qkv_sums[:, 1],
+        sums[0],
+        sums[1],
         d_w_qkv,
         d_qv_bias,
         d_w_out.astype(f32),
-        up_sums[:, 2],
-        up_sums[:, 0],
-        up_sums[:, 1],
-        d_w_up,
+        sums[4],
+        sums[2],
+        sums[3],
+        d_w_up.astype(f32),
         d_up_bias,
         d_w_down.astype(f32),
-        up_sums[:, 3],
+        sums[5],
     )
 
 

time: 532 us -> 535 us (level)
  blocking collectives: 84.6 us -> 29.8 us
  waiting for transfers between devices: 221 us -> 266 us
  starting transfers between devices: 22.5 us -> 39 us
  local copies, waits for them, and re-layouts: 53 us -> 42 us
  other arithmetic: 38.7 us -> 44.4 us
    all_to_all x5 -> x2, blocking collectives: 84.6 us -> 29.8 us  [exchange(): lax.all_to_all(rows, axis_name, split_axis=0, concat_axis=0, tiled=True)]
    all_to_all x5 -> x9, waiting for transfers between devices: 65.1 us -> 105 us  [exchange(): lax.all_to_all(rows, axis_name, split_axis=0, concat_axis=0, tiled=True)]
    psum x1, waiting for transfers between devices: 28.2 us -> 0.02 us  [local(): d_w_out = lax.psum(dot_tn(attended, grad_branch), 'ctx')]
    all_gather x6 -> x7, waiting for transfers between devices: 50.2 us -> 76.2 us  [gather(): return lax.all_gather(rows, axis_name, axis=0, tiled=True)]
    all_to_all x5 -> x9, starting transfers between devices: 21.6 us -> 38.4 us  [exchange(): lax.all_to_all(rows, axis_name, split_axis=0, concat_axis=0, tiled=True)]
    reduce_scatter x4, waiting for transfers between devices: 53.1 us -> 60 us  [scatter(): lax.psum_scatter(rows.astype(b16), 'fsdp', scatter_dimension=0, tiled=True)]
    slice x4 -> x6, local copies, waits for them, and re-layouts: 10.6 us -> 4.86 us  [the longest x1 3.47 us: own_row_sums(): return (whole[:, :groups * total], whole[:, groups * total:], ahead)]
  transfers between devices with their start and end apart: 18 -> 23, of which waited for: 12 -> 17; matrix products, arithmetic and copies ran while one was open for 14% -> 15% of each run, Pallas kernels for 12% -> 12%
where the time goes in v3:
time: 535 us; the launch traced here: 533 us
  waiting for transfers between devices  266 us (50%)
  Pallas kernels  62.7 us (12%)
  other arithmetic  44.4 us (8%)
  local copies, waits for them, and re-layouts  42 us (8%)
  starting transfers between devices  39 us (7%)
  matrix products  33.4 us (6%)
  blocking collectives  29.8 us (6%)
  between operations  14.6 us (3%)
    all_to_all x9, waiting for transfers between devices, exchange(): lax.all_to_all(rows, axis_name, split_axis=0, concat_axis=0, tiled=True)  105 us
    all_gather x7, waiting for transfers between devices, gather(): return lax.all_gather(rows, axis_name, axis=0, tiled=True)  76.2 us
    reduce_scatter x4, waiting for transfers between devices, scatter(): lax.psum_scatter(rows.astype(b16), 'fsdp', scatter_dimension=0, tiled=True)  60 us
    all_to_all x9, starting transfers between devices, exchange(): lax.all_to_all(rows, axis_name, split_axis=0, concat_axis=0, tiled=True)  38.4 us
    pallas_call x1, Pallas kernels, attend_back(): pl.pallas_call(functools.partial(attend_back_kernel, block_span), out_sha...  36.8 us
    all_to_all x2, blocking collectives, exchange(): lax.all_to_all(rows, axis_name, split_axis=0, concat_axis=0, tiled=True)  29.8 us
    pallas_call x1, Pallas kernels, attend(): pl.pallas_call(functools.partial(attend_kernel, block_span), out_shape=(j...  25.9 us
    all_gather x2, waiting for transfers between devices, own_columns(): whole = lax.all_gather(cut_cols, 'ctx', axis=0)  22.8 us
  transfers between devices with their start and end apart: 23, of which 17 were waited for; matrix products, arithmetic and copies ran while one was open for 15% of the time, Pallas kernels for 12%

profile of v3, /device:TPU:0, one launch (start us, length us, event | category | flops | bytes accessed | tf_op | source)
XLA Modules:
  0.0 532.5 jit_solution(4242961581145004946)
XLA Ops:
  11.4 1.7 fusion.27
  14.9 6.3 %all-to-all-start = ((bf16[4,32,768]{2,1,0:T(8,128)(2,1)}), bf16[4,32,768]{2,1,0:T(8,128)(2,1)S(1)}, u32[]{:S(2)}, u32[]{:S(2)}) async-start(bf16[4,32,768]{2,1,0:T(8,128)(2,1)} %copy.155), calls=%async_computation | async-start | bytes 393216 | tf_op jit(solution)/shard_map/all_to_all | solution.py:313
  22.3 9.3 %all-to-all-done = bf16[4,32,768]{2,1,0:T(8,128)(2,1)S(1)} async-done(((bf16[4,32,768]{2,1,0:T(8,128)(2,1)}), bf16[4,32,768]{2,1,0:T(8,128)(2,1)S(1)}, u32[]{:S(2)}, u32[]{:S(2)}) %all-to-all-start) | async-done | bytes 196640 | tf_op jit(solution)/shard_map/all_to_all | solution.py:313
  32.5 19.5 %all_to_all.55 = bf16[4,32,1024]{2,1,0:T(8,128)(2,1)} all-to-all(bf16[4,32,1024]{2,1,0:T(8,128)(2,1)S(1)} %copy.159), channel_id=1, replica_groups=mesh['ctx'=8,'fsdp'=4] {'fsdp'}, dimensions={0} | all-to-all | bytes 524288 | tf_op jit(solution)/shard_map/all_to_all | solution.py:313
  54.5 1.4 convert_reduce_fusion.2
  56.0 1.6 multiply_reduce_fusion
  58.1 22.8 %all-gather.26.cloned.1.call-done = bf16[32,32,768]{2,1,0:T(8,128)(2,1)} async-done(((bf16[4,32,768]{2,1,0:T(8,128)(2,1)}), bf16[32,32,768]{2,1,0:T(8,128)(2,1)}) %all-gather.26.cloned.1.call-update) | async-done | bytes 1572880 | tf_op jit(solution)/shard_map/all_gather | solution.py:355
  80.9 1.5 copy.156
  83.6 1.9 add_convert_fusion.1
  85.5 2.7 reshape.327
  90.5 3.6 all-to-all-start.1
  95.1 22.8 %all-to-all-done.1 = bf16[8,2,320,128]{3,2,1,0:T(8,128)(2,1)S(1)} async-done(((bf16[8,2,320,128]{3,2,1,0:T(8,128)(2,1)}), bf16[8,2,320,128]{3,2,1,0:T(8,128)(2,1)S(1)}, u32[]{:S(2)}, u32[]{:S(2)}) %all-to-all-start.1) | async-done | bytes 1310752 | tf_op jit(solution)/shard_map/all_to_all | solution.py:313
  117.9 25.9 %attend.1 = (bf16[16,64,128]{2,1,0:T(8,128)(2,1)S(1)}, f32[64,2048]{1,0:T(8,128)S(1)}, f32[1,2048]{1,0:T(1,128)S(1)}) custom-call(s32[16]{0:T(128)S(1)} %select_reduce_fusion.slots, s32[1]{0:T(128)} %bitcast.1.part, f32[1]{0:T(128)} %dynamic_slice.9.slope, bf16[16,320,128]{2,1,0:T(8,128)(2,1)S(1)} %bitcast.144), custom_call_target="tpu_custom_call" | custom-call | flops 2147483648 | bytes 2621440 | tf_op jit(solution)/shard_map/attend/pallas_call | solution.py:216
  145.3 3.2 copy.160
  148.5 10.3 %all_to_all.56 = bf16[8,2,64,128]{3,2,1,0:T(8,128)(2,1)S(1)} all-to-all(bf16[8,2,64,128]{3,2,1,0:T(8,128)(2,1)} %bitcast.147), channel_id=1, replica_groups=mesh['ctx'=8,'fsdp'=4] {'ctx'}, dimensions={0} | all-to-all | bytes 524288 | tf_op jit(solution)/shard_map/all_to_all | solution.py:313
  160.2 2.2 reshape.334
  162.4 2.5 convolution_convert_fusion.6
  165.0 26.4 %reduce-scatter.5.cloned.1.call-done = bf16[128,1024]{1,0:T(8,128)(2,1)} async-done(((bf16[512,1024]{1,0:T(8,128)(2,1)}), bf16[128,1024]{1,0:T(8,128)(2,1)}) %reduce-scatter.5.cloned.1.call-update) | async-done | bytes 262160 | tf_op jit(solution)/shard_map/reduce_scatter | solution.py:316
  193.8 1.9 add_convert_fusion.3
  196.0 26.5 %all-gather.16.cloned.1.call-done = bf16[512,1024]{1,0:T(8,128)(2,1)} async-done(((bf16[128,1024]{1,0:T(8,128)(2,1)}), bf16[512,1024]{1,0:T(8,128)(2,1)}) %all-gather.16.cloned.1.call-update) | async-done | bytes 1048592 | tf_op jit(solution)/shard_map/all_gather | solution.py:310
  222.4 3.2 fusion.38
  225.7 2.9 convert_reduce_fusion.1
  229.6 2.3 convolution_convert_fusion.3
  231.9 4.8 convolution_convert_fusion.1
  236.7 4.3 all-to-all-start.4
  241.1 2.8 convolution_convert_fusion
  243.9 1.5 copy.191
  245.4 13.3 %reduce-scatter.7.cloned.1.call-done = bf16[128,1024]{1,0:T(8,128)(2,1)} async-done(((bf16[512,1024]{1,0:T(8,128)(2,1)}), bf16[128,1024]{1,0:T(8,128)(2,1)}) %reduce-scatter.7.cloned.1.call-update) | async-done | bytes 262160 | tf_op jit(solution)/shard_map/reduce_scatter | solution.py:316
  258.7 1.8 convert_element_type.176
  260.5 7.2 %all-to-all-done.4 = bf16[8,128,1024]{2,1,0:T(8,128)(2,1)} async-done(((bf16[8,128,1024]{2,1,0:T(8,128)(2,1)}), bf16[8,128,1024]{2,1,0:T(8,128)(2,1)}, u32[]{:S(2)}, u32[]{:S(2)}) %all-to-all-start.4) | async-done | bytes 2097184 | tf_op jit(solution)/shard_map/all_to_all | solution.py:313
  267.7 4.4 all-to-all-start.5
  272.2 1.5 multiply_reduce_fusion.1
  273.7 2.4 fusion.32
  276.2 4.1 convolution_convert_fusion.5
  280.3 2.8 reduce_sum.238
  283.0 15.7 %all-to-all-done.5 = bf16[8,4,32,1024]{3,2,1,0:T(8,128)(2,1)} async-done(((bf16[8,4,32,1024]{3,2,1,0:T(8,128)(2,1)}), bf16[8,4,32,1024]{3,2,1,0:T(8,128)(2,1)}, u32[]{:S(2)}, u32[]{:S(2)}) %all-to-all-start.5) | async-done | bytes 2097184 | tf_op jit(solution)/shard_map/all_to_all | solution.py:313
  298.8 5.4 %all-gather.18.cloned.1.call-done = bf16[512,1024]{1,0:T(8,128)(2,1)} async-done(((bf16[128,1024]{1,0:T(8,128)(2,1)}), bf16[512,1024]{1,0:T(8,128)(2,1)}) %all-gather.18.cloned.1.call-update) | async-done | bytes 1048592 | tf_op jit(solution)/shard_map/all_gather | solution.py:310
  304.2 2.6 convolution_convert_fusion.7
  309.9 3.7 all-to-all-start.6
  313.5 2.7 reduce_sum.239
  316.3 5.1 all-to-all-done.6
  321.4 4.0 all-to-all-start.7
  325.4 36.8 %attend_back.1 = bf16[16,320,128]{2,1,0:T(8,128)(2,1)} custom-call(s32[16]{0:T(128)S(1)} %select_reduce_fusion.slots, s32[1]{0:T(128)} %bitcast.1.part, f32[1]{0:T(128)} %dynamic_slice.9.slope, bf16[16,320,128]{2,1,0:T(8,128)(2,1)S(1)} %bitcast.145, bf16[16,64,128]{2,1,0:T(8,128)(2,1)S(1)} %bitcast.146, f32[64,2048]{1,0:T(8,128)S(1)} %copy-done.4, ...), custom_call_target="tpu_custom_call" | custom-call | flops 2684354560 | bytes 5242880 | tf_op jit(solution)/shard_map/attend_back/pallas_call | solution.py:246
  362.2 3.7 all-to-all-start.8
  366.0 1.7 copy.185
  368.0 18.9 %all-to-all-done.8 = bf16[8,2,320,128]{3,2,1,0:T(8,128)(2,1)S(1)} async-done(((bf16[8,2,320,128]{3,2,1,0:T(8,128)(2,1)}), bf16[8,2,320,128]{3,2,1,0:T(8,128)(2,1)S(1)}, u32[]{:S(2)}, u32[]{:S(2)}) %all-to-all-start.8) | async-done | bytes 1310752 | tf_op jit(solution)/shard_map/all_to_all | solution.py:313
  386.9 12.7 %all-gather.20.cloned.1.call-done = bf16[1024,1024]{1,0:T(8,128)(2,1)} async-done(((bf16[128,1024]{1,0:T(8,128)(2,1)}), bf16[1024,1024]{1,0:T(8,128)(2,1)}) %all-gather.20.cloned.1.call-update) | async-done | bytes 2097168 | tf_op jit(solution)/shard_map/all_gather | solution.py:310
  403.7 1.5 copy.168
  405.2 3.7 fusion.31
  409.8 2.2 convolution_convert_fusion.2
  412.0 1.4 fusion.13
  413.4 3.1 copy.170
  416.4 1.4 copy.171
  417.9 3.6 all-to-all-start.9
  422.2 25.8 %all-to-all-done.9 = bf16[8,4,32,896]{3,2,1,0:T(8,128)(2,1)S(1)} async-done(((bf16[8,4,32,896]{3,2,1,0:T(8,128)(2,1)}), bf16[8,4,32,896]{3,2,1,0:T(8,128)(2,1)S(1)}, u32[]{:S(2)}, u32[]{:S(2)}) %all-to-all-start.9) | async-done | bytes 1835040 | tf_op jit(solution)/shard_map/all_to_all | solution.py:313
  449.0 4.7 all-to-all-start.10
  454.8 6.9 %all-gather.22.cloned.1.call-done = bf16[256,4096]{1,0:T(8,128)(2,1)} async-done(((bf16[32,4096]{1,0:T(8,128)(2,1)}), bf16[256,4096]{1,0:T(8,128)(2,1)}) %all-gather.22.cloned.1.call-update) | async-done | bytes 2097168 | tf_op jit(solution)/shard_map/all_gather | solution.py:310
  464.0 4.2 convert_element_type.198
  468.3 2.5 convert_element_type.197
  470.8 20.3 %reduce-scatter.11.cloned.1.call-done = bf16[128,1024]{1,0:T(8,128)(2,1)} async-done(((bf16[512,1024]{1,0:T(8,128)(2,1)}), bf16[128,1024]{1,0:T(8,128)(2,1)}) %reduce-scatter.11.cloned.1.call-update) | async-done | bytes 262160 | tf_op jit(solution)/shard_map/reduce_scatter | solution.py:316
  492.3 2.0 fusion.23
  494.3 23.9 %all-gather.24.cloned.1.call-done = bf16[256,3200]{1,0:T(8,128)(2,1)} async-done(((bf16[32,3200]{1,0:T(8,128)(2,1)}), bf16[256,3200]{1,0:T(8,128)(2,1)}) %all-gather.24.cloned.1.call-update) | async-done | bytes 1638416 | tf_op jit(solution)/shard_map/all_gather | solution.py:310
  518.2 1.6 convert_element_type.195
  522.5 3.5 slice.172
  (191 shorter events, 39.3 us)
Async XLA Ops:
  7.2 218.5 %copy-start = (bf16[1024,1024]{1,0:T(8,128)(2,1)S(1)}, bf16[1024,1024]{1,0:T(8,128)(2,1)}, u32[]{:S(2)}) copy-start(bf16[1024,1024]{1,0:T(8,128)(2,1)} %param.29) | copy-start | bytes 6291460
  7.2 46.5 %all-gather.12.cloned.1.call-start = ((), (), s32[]{:S(2)}) async-start(), calls=%async_computation.15 | async-start | bytes 1474560 | tf_op jit(solution)/shard_map/all_gather | solution.py:310
  14.0 38.6 %copy-start.20 = (bf16[4,128]{1,0:T(4,128)(2,1)S(1)}, bf16[4,128]{1,0:T(4,128)(2,1)}, u32[]{:S(2)}) copy-start(bf16[4,128]{1,0:T(4,128)(2,1)} %param.22) | copy-start | bytes 3076
  14.9 16.8 %all-to-all-start = ((bf16[4,32,768]{2,1,0:T(8,128)(2,1)}), bf16[4,32,768]{2,1,0:T(8,128)(2,1)S(1)}, u32[]{:S(2)}, u32[]{:S(2)}) async-start(bf16[4,32,768]{2,1,0:T(8,128)(2,1)} %copy.155), calls=%async_computation | async-start | bytes 393216 | tf_op jit(solution)/shard_map/all_to_all | solution.py:313
  21.2 59.7 %all-gather.26.cloned.1.call-start = ((), (), s32[]{:S(2)}) async-start(), calls=%async_computation.27 | async-start | bytes 1769472 | tf_op jit(solution)/shard_map/all_gather | solution.py:355
  31.6 0.7 copy-start.17
  32.3 113.0 %all-gather.28.cloned.1.call-start = ((), (), s32[]{:S(2)}) async-start(), calls=%async_computation.28 | async-start | bytes 2359296 | tf_op jit(solution)/shard_map/all_gather | solution.py:355
  52.0 96.4 %all-gather.14.cloned.1.call-start = ((), (), s32[]{:S(2)}) async-start(), calls=%async_computation.16 | async-start | bytes 1310720 | tf_op jit(solution)/shard_map/all_gather | solution.py:310
  53.7 3.9 copy-start.7
  58.1 24.4 %copy-start.16 = (bf16[4,128,1024]{2,1,0:T(8,128)(2,1)}, bf16[4,128,1024]{2,1,0:T(8,128)(2,1)S(1)}, u32[]{:S(2)}) copy-start(bf16[4,128,1024]{2,1,0:T(8,128)(2,1)S(1)} %add_convert_fusion) | copy-start | bytes 3145732
  82.4 1.2 copy-start.14
  89.2 5.0 copy-start.22
  89.2 5.1 copy-start.24
  90.5 27.3 %all-to-all-start.1 = ((bf16[8,2,320,128]{3,2,1,0:T(8,128)(2,1)}), bf16[8,2,320,128]{3,2,1,0:T(8,128)(2,1)S(1)}, u32[]{:S(2)}, u32[]{:S(2)}) async-start(bf16[8,2,320,128]{3,2,1,0:T(8,128)(2,1)} %maximum_maximum_fusion), calls=%async_computation.1 | async-start | bytes 2621440 | tf_op jit(solution)/shard_map/all_to_all | solution.py:313
  94.1 97.2 %reduce-scatter.5.cloned.1.call-start = ((), (), s32[]{:S(2)}) async-start(), calls=%async_computation.17 | async-start | bytes 1310720 | tf_op jit(solution)/shard_map/reduce_scatter | solution.py:316
  143.8 0.7 copy-start.2
  144.5 0.8 copy-start.3
  162.4 33.6 %copy-start.21 = (bf16[1024]{0:T(1024)(128)(2,1)S(1)}, bf16[1024]{0:T(1024)(128)(2,1)}, u32[]{:S(2)}) copy-start(bf16[1024]{0:T(1024)(128)(2,1)} %param.28) | copy-start | bytes 6148
  164.9 57.5 %all-gather.16.cloned.1.call-start = ((), (), s32[]{:S(2)}) async-start(), calls=%async_computation.18 | async-start | bytes 1310720 | tf_op jit(solution)/shard_map/all_gather | solution.py:310
  195.7 63.0 %reduce-scatter.7.cloned.1.call-start = ((), (), s32[]{:S(2)}) async-start(), calls=%async_computation.19 | async-start | bytes 1310720 | tf_op jit(solution)/shard_map/reduce_scatter | solution.py:316
  222.4 3.3 copy-start.23
  225.7 2.9 copy-start.25
  225.7 3.9 copy-start.12
  228.6 1.0 copy-start.26
  236.7 31.0 %all-to-all-start.4 = ((bf16[8,128,1024]{2,1,0:T(8,128)(2,1)}), bf16[8,128,1024]{2,1,0:T(8,128)(2,1)}, u32[]{:S(2)}, u32[]{:S(2)}) async-start(bf16[8,128,1024]{2,1,0:T(8,128)(2,1)} %bitcast.167), calls=%async_computation.6 | async-start | bytes 4194304 | tf_op jit(solution)/shard_map/all_to_all | solution.py:313
  267.7 31.0 %all-to-all-start.5 = ((bf16[8,4,32,1024]{3,2,1,0:T(8,128)(2,1)}), bf16[8,4,32,1024]{3,2,1,0:T(8,128)(2,1)}, u32[]{:S(2)}, u32[]{:S(2)}) async-start(bf16[8,4,32,1024]{3,2,1,0:T(8,128)(2,1)} %bitcast.154), calls=%async_computation.7 | async-start | bytes 4194304 | tf_op jit(solution)/shard_map/all_to_all | solution.py:313
  272.1 32.0 %all-gather.18.cloned.1.call-start = ((), (), s32[]{:S(2)}) async-start(), calls=%async_computation.20 | async-start | bytes 1310720 | tf_op jit(solution)/shard_map/all_gather | solution.py:310
  276.2 91.8 %all-reduce.4.cloned.1.call-start = ((), (), s32[]{:S(2)}) async-start(), calls=%async_computation.22 | async-start | bytes 1048576 | tf_op jit(solution)/shard_map/psum | solution.py:447
  280.3 23.9 %copy-start.9 = (bf16[512,256]{1,0:T(8,128)(2,1)S(1)}, bf16[512,256]{1,0:T(8,128)(2,1)}, u32[]{:S(2)}) copy-start(bf16[512,256]{1,0:T(8,128)(2,1)} %reshape.334) | copy-start | bytes 786436
  283.0 25.0 %copy-start.18 = (bf16[256,1024]{1,0:T(8,128)(2,1)S(1)}, bf16[256,1024]{1,0:T(8,128)(2,1)}, u32[]{:S(2)}) copy-start(bf16[256,1024]{1,0:T(8,128)(2,1)} %param.23) | copy-start | bytes 1572868
  304.2 3.9 copy-start.15
  306.8 92.9 %all-gather.20.cloned.1.call-start = ((), (), s32[]{:S(2)}) async-start(), calls=%async_computation.21 | async-start | bytes 2359296 | tf_op jit(solution)/shard_map/all_gather | solution.py:310
  307.4 146.4 %reduce-scatter.9.cloned.1.call-start = ((), (), s32[]{:S(2)}) async-start(), calls=%async_computation.24 | async-start | bytes 1310720 | tf_op jit(solution)/shard_map/reduce_scatter | solution.py:316
  309.0 16.4 %copy-start.4 = (f32[64,2048]{1,0:T(8,128)S(1)}, f32[64,2048]{1,0:T(8,128)}, u32[]{:S(2)}) copy-start(f32[64,2048]{1,0:T(8,128)} %copy-done.3) | copy-start | bytes 1572868
  309.9 11.5 %all-to-all-start.6 = ((bf16[8,2,64,128]{3,2,1,0:T(8,128)(2,1)}), bf16[8,2,64,128]{3,2,1,0:T(8,128)(2,1)S(1)}, u32[]{:S(2)}, u32[]{:S(2)}) async-start(bf16[8,2,64,128]{3,2,1,0:T(8,128)(2,1)} %pad_maximum_fusion.1), calls=%async_computation.8 | async-start | bytes 524288 | tf_op jit(solution)/shard_map/all_to_all | solution.py:313
  321.4 40.9 %all-to-all-start.7 = ((bf16[4,32,1024]{2,1,0:T(8,128)(2,1)}), bf16[4,32,1024]{2,1,0:T(8,128)(2,1)}, u32[]{:S(2)}, u32[]{:S(2)}) async-start(bf16[4,32,1024]{2,1,0:T(8,128)(2,1)} %reduce_sum.239), calls=%async_computation.9 | async-start | bytes 524288 | tf_op jit(solution)/shard_map/all_to_all | solution.py:313
  362.2 5.5 %copy-start.10 = (bf16[1,2,1,64,1024]{4,3,2,1,0:T(8,128)(2,1)S(1)}, bf16[1,2,1,64,1024]{4,3,2,1,0:T(8,128)(2,1)}, u32[]{:S(2)}) copy-start(bf16[1,2,1,64,1024]{4,3,2,1,0:T(8,128)(2,1)} %param.31) | copy-start | bytes 786436
  362.2 24.7 %all-to-all-start.8 = ((bf16[8,2,320,128]{3,2,1,0:T(8,128)(2,1)}), bf16[8,2,320,128]{3,2,1,0:T(8,128)(2,1)S(1)}, u32[]{:S(2)}, u32[]{:S(2)}) async-start(bf16[8,2,320,128]{3,2,1,0:T(8,128)(2,1)} %bitcast.39), calls=%async_computation.10 | async-start | bytes 2621440 | tf_op jit(solution)/shard_map/all_to_all | solution.py:313
  365.9 95.7 %all-gather.22.cloned.1.call-start = ((), (), s32[]{:S(2)}) async-start(), calls=%async_computation.23 | async-start | bytes 2359296 | tf_op jit(solution)/shard_map/all_gather | solution.py:310
  402.3 2.9 copy-start.8
  417.9 30.2 %all-to-all-start.9 = ((bf16[8,4,32,896]{3,2,1,0:T(8,128)(2,1)}), bf16[8,4,32,896]{3,2,1,0:T(8,128)(2,1)S(1)}, u32[]{:S(2)}, u32[]{:S(2)}) async-start(bf16[8,4,32,896]{3,2,1,0:T(8,128)(2,1)} %copy.171), calls=%async_computation.11 | async-start | bytes 3670016 | tf_op jit(solution)/shard_map/all_to_all | solution.py:313
  421.5 69.6 %reduce-scatter.11.cloned.1.call-start = ((), (), s32[]{:S(2)}) async-start(), calls=%async_computation.25 | async-start | bytes 1310720 | tf_op jit(solution)/shard_map/reduce_scatter | solution.py:316
  422.2 40.2 %copy-start.5 = (bf16[1,2,1,64,1024]{4,3,2,1,0:T(8,128)(2,1)S(1)}, bf16[1,2,1,64,1024]{4,3,2,1,0:T(8,128)(2,1)}, u32[]{:S(2)}) copy-start(bf16[1,2,1,64,1024]{4,3,2,1,0:T(8,128)(2,1)} %param.16) | copy-start | bytes 786436
  449.0 13.9 %copy-start.19 = (bf16[256,1024]{1,0:T(8,128)(2,1)S(1)}, bf16[256,1024]{1,0:T(8,128)(2,1)}, u32[]{:S(2)}) copy-start(bf16[256,1024]{1,0:T(8,128)(2,1)} %all-reduce.4.cloned.1.call-done) | copy-start | bytes 1572868
  449.0 12.6 %all-to-all-start.10 = ((bf16[4,32,896]{2,1,0:T(8,128)(2,1)}), bf16[4,32,896]{2,1,0:T(8,128)(2,1)S(1)}, u32[]{:S(2)}, u32[]{:S(2)}) async-start(bf16[4,32,896]{2,1,0:T(8,128)(2,1)} %reduce_sum.249), calls=%async_computation.12 | async-start | bytes 458752 | tf_op jit(solution)/shard_map/all_to_all | solution.py:313
  453.8 64.4 %all-gather.24.cloned.1.call-start = ((), (), s32[]{:S(2)}) async-start(), calls=%async_computation.26 | async-start | bytes 1843200 | tf_op jit(solution)/shard_map/all_gather | solution.py:310
  464.0 4.2 copy-start.11
  468.3 24.0 %copy-start.6 = (bf16[128,1024]{1,0:T(8,128)(2,1)S(1)}, bf16[128,1024]{1,0:T(8,128)(2,1)}, u32[]{:S(2)}) copy-start(bf16[128,1024]{1,0:T(8,128)(2,1)} %reduce-scatter.5.cloned.1.call-done) | copy-start | bytes 786436
  468.3 24.0 %copy-start.13 = (f32[128,1024]{1,0:T(8,128)S(1)}, f32[128,1024]{1,0:T(8,128)}, u32[]{:S(2)}) copy-start(f32[128,1024]{1,0:T(8,128)} %get-tuple-element.186) | copy-start | bytes 1572868
  521.9 4.1 copy-start.1
Sparse Core Ops, SparseCore 0:
  13.2 40.4 all-gather.11
  56.1 24.7 all-gather.25
  82.8 33.5 all-gather.27
  117.8 30.1 all-gather.13
  165.1 26.2 reduce-scatter.4
  195.8 26.5 all-gather.15
  232.0 26.6 reduce-scatter.6
  276.3 27.8 all-gather.17
  307.8 55.6 all-reduce.3
  366.0 33.5 all-gather.19
  402.6 27.1 reduce-scatter.8
  432.1 29.4 all-gather.21
  463.9 27.1 reduce-scatter.10
  493.6 24.6 all-gather.23
